TPU v7x, 512 devices: a whole 4x4x16 slice. The times are simulated.
512 devices in a mesh: ctx: 16 (over x, z_hi, core), exp: 32 (over y, z_lo).
Axes of the slice: x: 4, y: 4, z: 16 (z_hi: 2, z_lo: 8; z = z_hi * 8 + z_lo), core: 2. Of those that a mesh axis runs over, the one named last changes fastest.
Arguments:
- queries: bfloat16 [32, 2048, 2048], P('exp', 'ctx'), may hold values from -6 to 6
- keys: bfloat16 [32, 2048, 256], P('exp', 'ctx'), may hold values from -6 to 6
- values: bfloat16 [32, 2048, 256], P('exp', 'ctx'), may hold values from -6 to 6
- segments: int32 [32, 2048], P('exp', 'ctx'), may hold values from 0 to 7, never falling along the last dimension, each value on 1 to 1024 neighbouring positions
- residual: bfloat16 [32, 2048, 2048], P('exp', 'ctx'), may hold values from -6 to 6
- norm_gain: bfloat16 [2048], replicated, may hold values from 0.25 to 1.75
- expert_ids: int32 [32, 2048, 8], P('exp', 'ctx'), may hold values from 0 to 31, all different within a row; in each aligned block of 128 rows (0 to 127, 128 to 255, ..., all dimensions but the last counted through in order) at most 36 rows name the same one
- gate_weights: float32 [32, 2048, 8], P('exp', 'ctx'), may hold values from 0.1 to 1
- w_gate: bfloat16 [32, 2048, 384], P('exp', 'ctx'), may hold values from -0.125 to 0.125
- w_up: bfloat16 [32, 2048, 384], P('exp', 'ctx'), may hold values from -0.125 to 0.125
- w_down: bfloat16 [32, 384, 2048], P('exp', None, 'ctx'), may hold values from -0.3125 to 0.3125
Outputs:
- layer_out: bfloat16 [32, 2048, 2048], P('exp', 'ctx')
Inputs may be any that keep to these rules, and one draw needn't show every extreme that they name: `expert_ids`: each row names 8 different experts. Among the rows of one device (aligned blocks of 128 rows) no expert is named more than 36 times, and some device reaches 36. `segments`: within a sequence the ids never fall; each document has 1 to 1024 positions and one has exactly 1024.
All inputs are finite; a program needn't handle non-finite values.
Results may differ from a plain program's by a relative error of at most 0.0085.
Values may be sent and summed in bfloat16 or wider, within the bound.
No kernel may reach another device: no remote copies, remote signals or barrier semaphores. Data moves between devices by JAX's collectives and lax.ppermute only.
A program may use at most 64 MiB of HBM per device.

v0:
```python
import math

import jax
import jax.numpy as jnp
from jax import lax
from jax.sharding import PartitionSpec as P

D = 2048
HEADS = 16
KVH = 2
HD = 128
EXPERTS = 32
TOPK = 8
CAP = 36


def body(
    queries,
    keys,
    values,
    segments,
    residual,
    norm_gain,
    expert_ids,
    gate_weights,
    w_gate,
    w_up,
    w_down,
):
    rows_dev = queries.shape[1]
    groups = HEADS // KVH
    score_scale = HD ** (-0.5)
    row_offset = lax.axis_index("ctx") * rows_dev
    own_positions = row_offset + jnp.arange(rows_dev, dtype=jnp.int32)
    own_segments = segments[0].astype(jnp.bfloat16)
    query_block = jnp.transpose(queries[0].reshape(rows_dev, KVH, groups, HD), (1, 2, 0, 3))
    all_keys, all_values, all_segments = (
        lax.all_gather(keys, "ctx", axis=1, tiled=True),
        lax.all_gather(values, "ctx", axis=1, tiled=True),
        lax.all_gather(segments.astype(jnp.bfloat16), "ctx", axis=1, tiled=True),
    )
    seq_length = all_keys.shape[1]
    block = math.gcd(seq_length, 512)
    block_count = seq_length // block
    key_blocks = all_keys[0].reshape(block_count, block, KVH, HD)
    value_blocks = all_values[0].reshape(block_count, block, KVH, HD)
    segment_blocks = all_segments[0].reshape(block_count, block)

    def add_block(carry, inputs):
        key_block, value_block, segment_block, block_number = inputs
        key_positions = block_number * block + jnp.arange(block, dtype=jnp.int32)
        allowed = (own_segments[:, None] == segment_block[None, :]) & (
            key_positions[None, :] <= own_positions[:, None]
        )
        peak_score, denominator, accumulated = carry
        raw_scores = jnp.einsum(
            "gjtd,sgd->gjts", query_block, key_block, preferred_element_type=jnp.float32
        )
        masked = jnp.where(allowed, raw_scores * score_scale, -1e30)
        new_peak = jnp.maximum(peak_score, jnp.max(masked, axis=-1))
        weights = jnp.where(allowed, jnp.exp(masked - new_peak[..., None]), 0.0)
        rescale = jnp.exp(peak_score - new_peak)
        denominator = denominator * rescale + jnp.sum(weights, axis=-1)
        accumulated = accumulated * rescale[..., None] + jnp.einsum(
            "gjts,sgd->gjtd",
            weights.astype(jnp.bfloat16),
            value_block,
            preferred_element_type=jnp.float32,
        )
        return ((new_peak, denominator, accumulated), None)

    initial = (
        jnp.full((KVH, groups, rows_dev), -1e30, jnp.float32),
        jnp.zeros((KVH, groups, rows_dev), jnp.float32),
        jnp.zeros((KVH, groups, rows_dev, HD), jnp.float32),
    )
    final_state, unused_out = lax.scan(
        add_block,
        initial,
        (key_blocks, value_blocks, segment_blocks, jnp.arange(block_count, dtype=jnp.int32)),
    )
    peak_score, denominator, accumulated = final_state
    attended = jnp.transpose(accumulated / denominator[..., None], (2, 0, 1, 3)).reshape(
        rows_dev, HEADS * HD
    )
    hidden_state = residual[0].astype(jnp.float32) + attended
    normed = (
        hidden_state
        * lax.rsqrt(jnp.mean(hidden_state * hidden_state, axis=-1, keepdims=True) + 1e-06)
        * norm_gain.astype(jnp.float32)
    ).astype(jnp.bfloat16)
    exp_count = lax.axis_size("exp")
    per_dev = EXPERTS // exp_count
    flat_ids = expert_ids[0].reshape(-1)
    flat_gates = gate_weights[0].reshape(-1)
    owners = jnp.arange(rows_dev * TOPK, dtype=jnp.int32) // TOPK
    one_hot = (flat_ids[:, None] == jnp.arange(EXPERTS, dtype=jnp.int32)[None, :]).astype(jnp.int32)
    before = jnp.sum((jnp.cumsum(one_hot, axis=0) - one_hot) * one_hot, axis=1)
    slot_index = flat_ids * CAP + before
    outgoing = jnp.zeros((EXPERTS * CAP, D), jnp.bfloat16).at[slot_index].set(normed[owners])
    outgoing = outgoing.reshape(exp_count, per_dev, CAP, D)
    gate_all, up_all, down_all = (
        lax.all_gather(w_gate, "ctx", axis=1, tiled=True),
        lax.all_gather(w_up, "ctx", axis=1, tiled=True),
        lax.all_gather(w_down, "ctx", axis=2, tiled=True),
    )
    arrived = lax.all_to_all(outgoing, "exp", split_axis=0, concat_axis=0, tiled=True)
    gate_value = jnp.einsum("secd,edf->secf", arrived, gate_all, preferred_element_type=jnp.float32)
    upward = jnp.einsum("secd,edf->secf", arrived, up_all, preferred_element_type=jnp.float32)
    inner_act = (jax.nn.silu(gate_value) * upward).astype(jnp.bfloat16)
    expert_out = jnp.einsum(
        "secf,efd->secd", inner_act, down_all, preferred_element_type=jnp.float32
    ).astype(jnp.bfloat16)
    returned = lax.all_to_all(expert_out, "exp", split_axis=0, concat_axis=0, tiled=True)
    picked = returned.reshape(EXPERTS * CAP, D)[slot_index]
    routed = jnp.sum(
        picked.reshape(rows_dev, TOPK, D).astype(jnp.float32)
        * flat_gates.reshape(rows_dev, TOPK)[..., None],
        axis=1,
    )
    return (hidden_state + routed).astype(jnp.bfloat16)[None]


def solution(mesh):
    return jax.shard_map(
        body,
        mesh=mesh,
        in_specs=(
            P("exp", "ctx", None),
            P("exp", "ctx", None),
            P("exp", "ctx", None),
            P("exp", "ctx"),
            P("exp", "ctx", None),
            P(),
            P("exp", "ctx", None),
            P("exp", "ctx", None),
            P("exp", "ctx", None),
            P("exp", "ctx", None),
            P("exp", None, "ctx"),
        ),
        out_specs=P("exp", "ctx", None),
        check_vma=False,
    )
```

profile of v0, /device:TPU:1, one launch (start us, length us, event | category | flops | bytes accessed | tf_op | source)
XLA Modules:
  0.0 866.8 jit_solution(12249096240002973047)
XLA Ops:
  9.7 50.5 %all_gather.18 = bf16[1,2048]{1,0:T(2,128)(2,1)S(1)} all-gather(bf16[1,128]{1,0:T(2,128)(2,1)S(1)} %get-tuple-element.156), channel_id=1, replica_groups=mesh['ctx'=16,'exp'=32] {'ctx'}, dimensions={1}, use_global_device_ids=true | all-gather | bytes 4352 | tf_op jit(solution)/shard_map/all_gather | solution.py:40
  64.3 9.0 %reduce-window.6 = s32[32,8,128]{2,1,0:T(8,128)S(1)} reduce-window(s32[32,8,128]{2,1,0:T(8,128)S(1)} %fusion.54, s32[]{:T(128)} %constant.58.clone.1), window={size=1x1x128 pad=0_0x0_0x127_0}, to_apply=%region_4.5 | reduce-window | flops 4161536 | bytes 262148 | tf_op jit(solution)/shard_map/reduce-window
  74.1 20.1 %all-gather.6.cloned.1.call-done = bf16[1,2048,256]{2,1,0:T(8,128)(2,1)} async-done(((bf16[1,128,256]{2,1,0:T(8,128)(2,1)}), bf16[1,2048,256]{2,1,0:T(8,128)(2,1)}) %all-gather.6.cloned.1.call-update) | async-done | bytes 1048592 | tf_op jit(solution)/shard_map/all_gather | solution.py:38
  94.1 1.3 reshape_squeeze.14
  95.5 70.5 %all-gather.8.cloned.1.call-done = bf16[1,2048,256]{2,1,0:T(8,128)(2,1)} async-done(((bf16[1,128,256]{2,1,0:T(8,128)(2,1)}), bf16[1,2048,256]{2,1,0:T(8,128)(2,1)}) %all-gather.8.cloned.1.call-update) | async-done | bytes 1048592 | tf_op jit(solution)/shard_map/all_gather | solution.py:39
  167.4 45.7 %while.15 = (s32[]{:T(128)}, f32[2,8,128]{2,1,0:T(8,128)S(1)}, f32[2,8,128]{2,1,0:T(8,128)S(1)}, f32[2,8,128,128]{3,2,1,0:T(8,128)}, bf16[128]{0:T(256)(128)(2,1...) while((s32[]{:T(128)}, f32[2,8,128]{2,1,0:T(8,128)S(1)}, ...), condition=%wide.region_3.4_spmd.clone, body=%wide.region_0.3_spmd.clone.sunk | while | flops 551627392 | bytes 33956308 | solution.py:77
  169.3 2.7 fusion.66
  171.9 3.3 fusion.67
  175.4 2.5 fusion.69
  179.8 2.7 fusion.66
  182.5 3.3 fusion.67
  185.9 3.7 fusion.69
  191.5 2.7 fusion.66
  194.2 3.3 fusion.67
  197.6 3.7 fusion.69
  203.2 2.7 fusion.66
  205.9 3.3 fusion.67
  209.4 3.7 fusion.69
  213.1 2.2 fusion.49
  216.4 23.0 %scatter_custom_fusion = bf16[1152,2048]{1,0:T(8,128)(2,1)} fusion(s32[1024]{0:T(1024)S(1)} %bitcast.179, bf16[128,2048]{1,0:T(8,128)(2,1)S(1)} %fusion.47, s32[1024]{0:T(1024)S(1)} %broadcast_clamp_fusion.1, bf16[]{:T(256)} %constant.64.clone.1), kind=kCustom, calls=%fused_computation.36 | custom fusion | bytes 4718594 | tf_op jit(solution)/shard_map/scatter | solution.py:100
  239.4 7.2 reshape.154
  246.6 5.1 all-to-all-start
  253.7 118.1 %all-gather.10.cloned.1.call-done = bf16[1,2048,384]{2,1,0:T(8,128)(2,1)} async-done(((bf16[1,128,384]{2,1,0:T(8,128)(2,1)}), bf16[1,2048,384]{2,1,0:T(8,128)(2,1)}) %all-gather.10.cloned.1.call-update) | async-done | bytes 1572880 | tf_op jit(solution)/shard_map/all_gather | solution.py:103
  371.8 142.2 %all-to-all-done = bf16[32,1,36,2048]{3,2,1,0:T(8,128)(2,1)} async-done(((bf16[32,1,36,2048]{3,2,1,0:T(8,128)(2,1)}), bf16[32,1,36,2048]{3,2,1,0:T(8,128)(2,1)}, u32[]{:S(2)}, u32[]{:S(2)}) %all-to-all-start) | async-done | bytes 4718624 | tf_op jit(solution)/shard_map/all_to_all | solution.py:107
  514.0 7.1 fusion.19
  521.1 75.0 %all-gather.14.cloned.1.call-done = bf16[1,384,2048]{2,1,0:T(8,128)(2,1)} async-done(((bf16[1,384,128]{2,1,0:T(8,128)(2,1)}), bf16[1,384,2048]{2,1,0:T(8,128)(2,1)}) %all-gather.14.cloned.1.call-update) | async-done | bytes 1572880 | tf_op jit(solution)/shard_map/all_gather | solution.py:105
  596.1 10.4 %convert_bitcast_fusion = bf16[32,1,36,2048]{3,2,1,0:T(8,128)(2,1)} fusion(bf16[1,384,2048]{2,1,0:T(8,128)(2,1)} %all-gather.14.cloned.1.call-done, bf16[1,2048,384]{2,1,0:T(8,128)(2,1)} %all-gather.12.cloned.1.call-done, bf16[32,1,36,2048]{3,2,1,0:T(8,128)(2,1)} %all-to-all-done, f32[32,36,384]{2,1,0:T(8,128)} %fusion.19), kind=kOutput, calls=%fused_computation.35 | convolution fusion | flops 3628892160 | bytes 14352384 | tf_op jit(solution)/shard_map/secf,efd->secd/dot_general | solution.py:111
  606.5 5.0 all-to-all-start.1
  611.8 221.9 %all-to-all-done.1 = bf16[32,1,36,2048]{3,2,1,0:T(8,128)(2,1)} async-done(((bf16[32,1,36,2048]{3,2,1,0:T(8,128)(2,1)}), bf16[32,1,36,2048]{3,2,1,0:T(8,128)(2,1)}, u32[]{:S(2)}, u32[]{:S(2)}) %all-to-all-start.1) | async-done | bytes 4718624 | tf_op jit(solution)/shard_map/all_to_all | solution.py:114
  833.7 7.2 reshape.160
  840.9 11.8 %gather_fusion = bf16[1024,2048]{1,0:T(8,128)(2,1)} fusion(bf16[1152,2048]{1,0:T(8,128)(2,1)} %reshape.160, s32[1024]{0:T(1024)S(1)} %broadcast_clamp_fusion), kind=kCustom, calls=%fused_computation.1 | custom fusion | bytes 8392704 | tf_op jit(solution)/shard_map/gather | solution.py:115
  852.7 6.5 fusion.16
  (100 shorter events, 18.8 us)
Async XLA Ops:
  6.5 67.1 %copy-start.2 = (s32[1,128,8]{1,2,0:T(8,128)S(1)}, s32[1,128,8]{1,2,0:T(8,128)}, u32[]{:S(2)}) copy-start(s32[1,128,8]{1,2,0:T(8,128)} %param.19) | copy-start | bytes 12292
  6.5 57.7 %copy-start.3 = (bf16[2048]{0:T(1024)(128)(2,1)S(1)}, bf16[2048]{0:T(1024)(128)(2,1)}, u32[]{:S(2)}) copy-start(bf16[2048]{0:T(1024)(128)(2,1)} %param.18) | copy-start | bytes 12292
  6.5 87.6 %all-gather.6.cloned.1.call-start = ((), (), s32[]{:S(2)}) async-start(), calls=%async_computation.2 | async-start | bytes 1114112 | tf_op jit(solution)/shard_map/all_gather | solution.py:38
  7.3 158.7 %all-gather.8.cloned.1.call-start = ((), (), s32[]{:S(2)}) async-start(), calls=%async_computation.3 | async-start | bytes 1114112 | tf_op jit(solution)/shard_map/all_gather | solution.py:39
  171.9 3.4 copy-start
  182.4 3.4 copy-start
  194.2 3.4 copy-start
  205.9 3.4 copy-start
  213.1 2.8 copy-start.1
  246.6 267.4 %all-to-all-start = ((bf16[32,1,36,2048]{3,2,1,0:T(8,128)(2,1)}), bf16[32,1,36,2048]{3,2,1,0:T(8,128)(2,1)}, u32[]{:S(2)}, u32[]{:S(2)}) async-start(bf16[32,1,36,2048]{3,2,1,0:T(8,128)(2,1)} %bitcast.172), calls=%async_computation | async-start | bytes 10485760 | tf_op jit(solution)/shard_map/all_to_all | solution.py:107
  251.8 120.0 %all-gather.10.cloned.1.call-start = ((), (), s32[]{:S(2)}) async-start(), calls=%async_computation.4 | async-start | bytes 1671168 | tf_op jit(solution)/shard_map/all_gather | solution.py:103
  252.5 268.6 %all-gather.12.cloned.1.call-start = ((), (), s32[]{:S(2)}) async-start(), calls=%async_computation.5 | async-start | bytes 1671168 | tf_op jit(solution)/shard_map/all_gather | solution.py:104
  253.1 343.0 %all-gather.14.cloned.1.call-start = ((), (), s32[]{:S(2)}) async-start(), calls=%async_computation.6 | async-start | bytes 1671168 | tf_op jit(solution)/shard_map/all_gather | solution.py:105
  606.5 5.1 copy-start.4
  606.5 227.2 %all-to-all-start.1 = ((bf16[32,1,36,2048]{3,2,1,0:T(8,128)(2,1)}), bf16[32,1,36,2048]{3,2,1,0:T(8,128)(2,1)}, u32[]{:S(2)}, u32[]{:S(2)}) async-start(bf16[32,1,36,2048]{3,2,1,0:T(8,128)(2,1)} %convert_bitcast_fusion), calls=%async_computation.1 | async-start | bytes 10485760 | tf_op jit(solution)/shard_map/all_to_all | solution.py:114
Sparse Core Ops, SparseCore 0:
  10.6 83.4 all-gather.5
  97.4 68.5 all-gather.7
  255.9 115.8 all-gather.9
  374.9 129.8 all-gather.11
  507.8 88.2 all-gather.13
where the time goes:
time: 880 us; the launch traced here: 867 us
  waiting for transfers between devices  651 us (74%)
  local copies, waits for them, and re-layouts  61.4 us (7%)
  blocking collectives  50.5 us (6%)
  matrix products  41.9 us (5%)
  other arithmetic  35.6 us (4%)
  between operations  13.3 us (2%)
  starting transfers between devices  10.3 us (1%)
    all_to_all x1, waiting for transfers between devices, body(): lax.all_to_all(expert_out, 'exp', split_axis=0, concat_axis=0, tiled=True)  222 us
    all_to_all x1, waiting for transfers between devices, body(): lax.all_to_all(outgoing, 'exp', split_axis=0, concat_axis=0, tiled=True)  142 us
    all_gather x1, waiting for transfers between devices, body(): lax.all_gather(w_gate, 'ctx', axis=1, tiled=True)  118 us
    all_gather x1, waiting for transfers between devices, body(): lax.all_gather(w_down, 'ctx', axis=2, tiled=True)  75 us
    all_gather x1, waiting for transfers between devices, body(): lax.all_gather(values, 'ctx', axis=1, tiled=True)  70.5 us
    all_gather x1, blocking collectives, body(): lax.all_gather(segments.astype(jnp.bfloat16), 'ctx', axis=1, tiled=True)  50.5 us
    scatter x1, local copies, waits for them, and re-layouts, body(): jnp.zeros((EXPERTS * CAP, D), jnp.bfloat16).at[slot_index]  23 us
    all_gather x1, waiting for transfers between devices, body(): lax.all_gather(keys, 'ctx', axis=1, tiled=True)  20.1 us
  transfers between devices with their start and end apart: 7, of which 6 were waited for; matrix products, arithmetic and copies ran while one was open for 3% of the time, Pallas kernels for 0%

commit v1 on v0

v1 whole, which is shorter than its diff:
```python
import functools

import jax
import jax.numpy as jnp
from jax import lax
from jax.experimental import pallas as pl
from jax.experimental.pallas import tpu as pltpu
from jax.sharding import Mesh, PartitionSpec as P

D = 2048
HEADS = 16
KVH = 2
GROUPS = HEADS // KVH
HD = 128
FF = 384
EXPERTS = 32
TOPK = 8
TOK = 128
CAP = 36
SLOTS = EXPERTS * CAP
PACK = 144
WINDOW = 9
BLOCKS = 12
AXES = ("x", "zh", "c", "y", "zl")
F32 = jnp.float32
BF16 = jnp.bfloat16
NT = (((1,), (1,)), ((), ()))


def params(mib):
    return pltpu.CompilerParams(vmem_limit_bytes=mib * 1024 * 1024)


def slot_kernel(ids_ref, gates_ref, send_ref, high_ref, low_ref):
    ids = ids_ref[...]
    gates = gates_ref[...]
    column = lax.broadcasted_iota(jnp.int32, (TOK, EXPERTS), 1)
    named = jnp.zeros((TOK, EXPERTS), F32)
    gate = jnp.zeros((TOK, EXPERTS), F32)
    for k in range(TOPK):
        hit = ids[:, k : k + 1] == column
        named = named + jnp.where(hit, 1.0, 0.0)
        gate = gate + jnp.where(hit, gates[:, k : k + 1], 0.0)
    row = lax.broadcasted_iota(jnp.int32, (TOK, TOK), 0)
    earlier = (lax.broadcasted_iota(jnp.int32, (TOK, TOK), 1) < row).astype(F32).astype(BF16)
    rank = jnp.dot(earlier, named.astype(BF16), preferred_element_type=F32)
    rank = jnp.where(named > 0.0, rank, -1.0).astype(BF16)
    slot = lax.broadcasted_iota(jnp.int32, (SLOTS, EXPERTS), 0).astype(F32)
    owner = jnp.floor((slot + 0.5) * (1.0 / CAP))
    place = slot - CAP * owner
    expert = lax.broadcasted_iota(jnp.int32, (SLOTS, EXPERTS), 1).astype(F32)
    spread = jnp.where(owner == expert, 1.0, 0.0).astype(BF16)
    rank_rows = lax.dot_general(spread, rank, NT, preferred_element_type=F32)
    send_ref[...] = jnp.where(rank_rows == place[:, :1], 1.0, 0.0).astype(BF16)
    slot_t = lax.broadcasted_iota(jnp.int32, (1, SLOTS), 1).astype(F32)
    place_t = slot_t - CAP * jnp.floor((slot_t + 0.5) * (1.0 / CAP))
    taken = lax.dot_general(rank, spread, NT, preferred_element_type=F32) == place_t
    high = gate.astype(BF16)
    low = (gate - high.astype(F32)).astype(BF16)
    for part, ref in ((high, high_ref), (low, low_ref)):
        wide = lax.dot_general(part, spread, NT, preferred_element_type=F32)
        ref[...] = jnp.where(taken, wide, 0.0).astype(BF16)


def slot_matrices(ids, gates):
    return pl.pallas_call(
        slot_kernel,
        out_shape=(
            jax.ShapeDtypeStruct((SLOTS, TOK), BF16),
            jax.ShapeDtypeStruct((TOK, SLOTS), BF16),
            jax.ShapeDtypeStruct((TOK, SLOTS), BF16),
        ),
        compiler_params=params(32),
        cost_estimate=pl.CostEstimate(flops=40_000_000, bytes_accessed=1_000_000, transcendentals=0),
        name="slots",
    )(ids, gates)


def attention_kernel(where_ref, q_hbm, seg_ref, res_hbm, gain_ref, send_ref, *rest):
    blocks = rest[:BLOCKS]
    hidden_ref, out_ref, kv, segs, bias, hidden, q_ref, res_ref, sem = rest[BLOCKS:]
    q_in = pltpu.make_async_copy(q_hbm, q_ref, sem.at[0])
    res_in = pltpu.make_async_copy(res_hbm, res_ref, sem.at[1])
    q_in.start()
    res_in.start()
    x, zh, c = where_ref[0], where_ref[1], where_ref[2]
    index = 0
    for back in (2, 1, 0):
        for other_zh in (0, 1):
            for other_c in (0, 1):
                zh_at = zh if other_zh == 0 else 1 - zh
                c_at = c if other_c == 0 else 1 - c
                slot = (2 - back) * 4 + zh_at * 2 + c_at
                kv[pl.ds(pl.multiple_of(slot * TOK, TOK), TOK), :] = blocks[index][:TOK, :]
                row = blocks[index][TOK:, :TOK].astype(F32)
                segs[pl.ds(slot, 1), :] = row[:1, :]
                index += 1
    first = zh * 2 + c
    own = x * 4 + first
    mine = seg_ref[...]
    t = lax.broadcasted_iota(jnp.int32, (TOK, TOK), 0)
    s = lax.broadcasted_iota(jnp.int32, (TOK, TOK), 1)
    for i in range(WINDOW):
        number = own - (WINDOW - 1) + i
        same = segs[pl.ds(first + i, 1), :] == mine
        allowed = same & (number >= 0)
        if i == WINDOW - 1:
            allowed = allowed & (s <= t)
        bias[:, i * TOK : (i + 1) * TOK] = jnp.where(allowed, 0.0, -1e30)
    start = pl.multiple_of(first * TOK, TOK)
    rate = HD ** (-0.5) * 1.4426950408889634
    q_in.wait()
    res_in.wait()
    for g in range(KVH):
        key = kv[pl.ds(start, WINDOW * TOK), g * HD : (g + 1) * HD]
        value = kv[pl.ds(start, WINDOW * TOK), (KVH + g) * HD : (KVH + g + 1) * HD]
        for j in range(GROUPS):
            columns = slice((g * GROUPS + j) * HD, (g * GROUPS + j + 1) * HD)
            score = lax.dot_general(q_ref[:, columns], key, NT, preferred_element_type=F32)
            score = score + bias[...]
            peak = jnp.max(score, axis=-1, keepdims=True)
            weight = jnp.exp2((score - peak) * rate)
            total = jnp.sum(weight, axis=-1, keepdims=True)
            mixed = jnp.dot(weight.astype(BF16), value, preferred_element_type=F32)
            hidden[:, columns] = res_ref[:, columns].astype(F32) + mixed / total
    full = hidden[...]
    hidden_ref[...] = full
    mean = jnp.mean(full * full, axis=-1, keepdims=True)
    normed = (full * lax.rsqrt(mean + 1e-6) * gain_ref[...].astype(F32)).astype(BF16)
    for n in range(0, D, 512):
        out_ref[:, n : n + 512] = jnp.dot(
            send_ref[...], normed[:, n : n + 512], preferred_element_type=F32
        ).astype(BF16)


def attention(where, q, seg, res, gain, send, blocks):
    whole = pl.BlockSpec(memory_space=pltpu.VMEM)
    hbm = pl.BlockSpec(memory_space=pl.ANY)
    return pl.pallas_call(
        attention_kernel,
        in_specs=[pl.BlockSpec(memory_space=pltpu.SMEM), hbm, whole, hbm] + [whole] * (2 + BLOCKS),
        out_specs=(whole, whole),
        out_shape=(
            jax.ShapeDtypeStruct((TOK, D), F32),
            jax.ShapeDtypeStruct((SLOTS, D), BF16),
        ),
        scratch_shapes=[
            pltpu.VMEM((BLOCKS * TOK, 2 * KVH * HD), BF16),
            pltpu.VMEM((16, TOK), F32),
            pltpu.VMEM((TOK, WINDOW * TOK), F32),
            pltpu.VMEM((TOK, D), F32),
            pltpu.VMEM((TOK, D), BF16),
            pltpu.VMEM((TOK, D), BF16),
            pltpu.SemaphoreType.DMA((2,)),
        ],
        compiler_params=params(48),
        cost_estimate=pl.CostEstimate(
            flops=1_900_000_000, bytes_accessed=9_000_000, transcendentals=2_400_000
        ),
        name="attend",
    )(where, q, seg, res, gain, send, *blocks)


def slice_place(expert, x, zh, c):
    return (expert + 8 * zh + (x - 4 if c == 0 else 3 - x)) % 16


STEP = 576


def expert_kernel(where_ref, x_hbm, w_hbm, out_hbm, x_ref, w_ref, out_ref, sem_x, sem_w, sem_out):
    x = where_ref[0]
    chunks = range(0, SLOTS, STEP)

    def rows_in(i):
        at = pl.ds(i * STEP, STEP)
        return pltpu.make_async_copy(x_hbm.at[at], x_ref.at[at], sem_x.at[i])

    def rows_out(i):
        at = pl.ds(i * STEP, STEP)
        return pltpu.make_async_copy(out_ref.at[at], out_hbm.at[at], sem_out.at[i])

    def weight_slice(which, k):
        place = slice_place(2 * x + which, k // 4, (k // 2) % 2, k % 2)
        at = pl.ds(pl.multiple_of((which * 16 + place) * TOK, TOK), TOK)
        return pltpu.make_async_copy(
            w_hbm.at[at], w_ref.at[which, pl.ds(k * TOK, TOK)], sem_w.at[which, k]
        )

    rows_in(0).start()
    for which in (0, 1):
        for k in range(16):
            weight_slice(which, k).start()
        if which == 0:
            for i in range(1, len(chunks)):
                rows_in(i).start()

    def run(rows, which):
        gate_up = jnp.dot(rows, w_ref[which, :, : 2 * FF], preferred_element_type=F32)
        gate, up = gate_up[:, :FF], gate_up[:, FF:]
        inner = (gate * jax.nn.sigmoid(gate) * up).astype(BF16)
        return lax.dot_general(
            inner, w_ref[which, :, 2 * FF :], NT, preferred_element_type=F32
        ).astype(BF16)

    line = lax.broadcasted_iota(jnp.int32, (16, 1), 0)
    for which in (0, 1):
        for k in range(16):
            weight_slice(which, k).wait()
        for i, chunk in enumerate(chunks):
            starts = range(chunk, chunk + STEP, 144)
            if which == 0:
                rows_in(i).wait()
                rows = [x_ref[a + b : a + b + 48, :] for a in starts for b in (0, 96)]
                y = run(jnp.concatenate(rows, axis=0), 0)
                for n, a in enumerate(starts):
                    out_ref[a : a + 48, :] = y[n * 96 : n * 96 + 48]
                    out_ref[a + 96 : a + 144, :] = y[n * 96 + 48 : n * 96 + 96]
            else:
                y = run(jnp.concatenate([x_ref[a + 32 : a + 112, :] for a in starts], axis=0), 1)
                for n, a in enumerate(starts):
                    p = y[n * 80 : n * 80 + 80]
                    head, tail = out_ref[a + 32 : a + 48, :], out_ref[a + 96 : a + 112, :]
                    out_ref[a + 32 : a + 48, :] = jnp.where(line < 4, head, p[:16])
                    out_ref[a + 48 : a + 96, :] = p[16:64]
                    out_ref[a + 96 : a + 112, :] = jnp.where(line < 12, p[64:], tail)
                rows_out(i).start()
    for i in range(len(chunks)):
        rows_out(i).wait()


def experts(where, x, both):
    hbm = pl.BlockSpec(memory_space=pl.ANY)
    return pl.pallas_call(
        expert_kernel,
        in_specs=[pl.BlockSpec(memory_space=pltpu.SMEM), hbm, hbm],
        out_specs=hbm,
        out_shape=jax.ShapeDtypeStruct((SLOTS, D), BF16),
        scratch_shapes=[
            pltpu.VMEM((SLOTS, D), BF16),
            pltpu.VMEM((2, D, 3 * FF), BF16),
            pltpu.VMEM((SLOTS, D), BF16),
            pltpu.SemaphoreType.DMA((SLOTS // STEP,)),
            pltpu.SemaphoreType.DMA((2, 16)),
            pltpu.SemaphoreType.DMA((SLOTS // STEP,)),
        ],
        compiler_params=params(56),
        cost_estimate=pl.CostEstimate(
            flops=6_600_000_000, bytes_accessed=19_000_000, transcendentals=540_000
        ),
        name="expert_mlp",
    )(where, x, both)


def combine_kernel(hidden_ref, high_ref, low_ref, back_ref, out_ref):
    back = back_ref[...]
    routed = jnp.dot(high_ref[...], back, preferred_element_type=F32)
    routed = routed + jnp.dot(low_ref[...], back, preferred_element_type=F32)
    out_ref[...] = (hidden_ref[...] + routed).astype(BF16)


def combine(hidden, high, low, back):
    wide = 512
    return pl.pallas_call(
        combine_kernel,
        grid=(D // wide,),
        in_specs=[
            pl.BlockSpec((TOK, wide), lambda i: (0, i)),
            pl.BlockSpec((TOK, SLOTS), lambda i: (0, 0)),
            pl.BlockSpec((TOK, SLOTS), lambda i: (0, 0)),
            pl.BlockSpec((SLOTS, wide), lambda i: (0, i)),
        ],
        out_specs=pl.BlockSpec((TOK, wide), lambda i: (0, i)),
        out_shape=jax.ShapeDtypeStruct((TOK, D), BF16),
        compiler_params=params(32),
        cost_estimate=pl.CostEstimate(
            flops=1_200_000_000, bytes_accessed=7_000_000, transcendentals=0
        ),
        name="combine",
    )(hidden, high, low, back)


def shifted(steps, swap):
    return [
        (x * 2 + c, (x + steps) * 2 + (c ^ swap)) for x in range(4) for c in range(2) if x + steps < 4
    ]


def to_expert_column():
    pairs = []
    for k in range(16):
        for zl in range(8):
            place = slice_place(zl, k // 4, (k // 2) % 2, k % 2)
            target = ((zl // 2 * 2 + place // 8) * 2 + zl % 2) * 8 + place % 8
            pairs.append((k * 8 + zl, target))
    return pairs


def body(q, k, v, seg, res, gain, ids, gates, w_gate, w_up, w_down):
    x, zh, c, y = (lax.axis_index(a) for a in ("x", "zh", "c", "y"))
    swap = [(0, 1), (1, 0)]

    seg_rows = jnp.pad(seg.astype(BF16), ((0, PACK - TOK - 1), (0, 2 * KVH * HD - TOK)))
    packet = jnp.concatenate([jnp.concatenate([k[0], v[0]], axis=1), seg_rows], axis=0)
    def spread(source):
        found = [[source, lax.ppermute(source, "c", swap)]]
        for back in (1, 2):
            found.append([lax.ppermute(source, ("x", "c"), shifted(back, o)) for o in (0, 1)])
        return found

    packet_zh = lax.ppermute(packet, "zh", swap)
    near = spread(packet)
    packed = jnp.concatenate([w_gate[0], w_up[0], w_down[0].T], axis=1)
    packed = lax.ppermute(packed, ("x", "zh", "c", "zl"), to_expert_column())
    packed, packet_zh, near = lax.optimization_barrier((packed, packet_zh, near))
    both = lax.all_gather(packed, ("c", "zh", "zl"), axis=0, tiled=True)
    far = spread(packet_zh)
    blocks = [side[b][o] for b in (2, 1, 0) for side in (near, far) for o in (0, 1)]

    e = ids[0]
    half = (e & 1) ^ (y & 1)
    order = ((e >> 1) & 3) * 8 + (e >> 3) * 2 + half
    send, high, low = slot_matrices(order, gates[0])

    where = jnp.stack([x, zh, c]).astype(jnp.int32)
    hidden, outgoing = attention(
        where, q[0], seg[0].astype(F32)[:, None], res[0], gain[None], send, blocks
    )
    arrived = lax.all_to_all(outgoing, ("x", "y"), 0, 0, tiled=True)
    done = experts(where, arrived, both)
    back = lax.all_to_all(done, ("x", "y"), 0, 0, tiled=True)
    return combine(hidden, high, low, back)[None]


def solution(mesh):
    fine = Mesh(mesh.devices.reshape(4, 2, 2, 4, 8), AXES)
    exp, ctx = ("y", "zl"), ("x", "zh", "c")
    rows = P(exp, ctx, None)
    return jax.shard_map(
        body,
        mesh=fine,
        in_specs=(rows, rows, rows, P(exp, ctx), rows, P(), rows, rows, rows, rows, P(exp, None, ctx)),
        out_specs=rows,
        check_vma=False,
    )
```

time: 880 us -> 239 us (0.27); the launches traced: 867 us -> 238 us
  waiting for transfers between devices: 651 us -> 14.9 us
  blocking collectives: 50.5 us -> 122 us
  local copies, waits for them, and re-layouts: 61.4 us -> 6.45 us
  matrix products: 41.9 us -> 0 us
  starting transfers between devices: 10.3 us -> 44.2 us
  Pallas kernels: 0 us -> 32.2 us
  other arithmetic: 35.6 us -> 4.09 us
    all_to_all x2 -> x0, waiting for transfers between devices: 364 us -> none  [the longest x1 222 us: body(): lax.all_to_all(expert_out, 'exp', split_axis=0, concat_axis=0, tiled=True)]
    all_gather x5 -> x1, waiting for transfers between devices: 284 us -> 0.01 us  [body(): both = lax.all_gather(packed, ('c', 'zh', 'zl'), axis=0, tiled=True)]
    all_to_all x0 -> x2, blocking collectives: none -> 122 us  [the longest x1 63.9 us: body(): arrived = lax.all_to_all(outgoing, ('x', 'y'), 0, 0, tiled=True)]
    all_gather x1 -> x0, blocking collectives: 50.5 us -> none  [body(): lax.all_gather(segments.astype(jnp.bfloat16), 'ctx', axis=1, tiled=True)]
    ppermute x0 -> x12, starting transfers between devices: none -> 44.2 us  [the longest x8 19.7 us: spread(): lax.ppermute(source, ('x', 'c'), shifted(back, o))]
    dot_general x10 -> x0, matrix products: 41.9 us -> none  [the longest x4 13.7 us: add_block(): jnp.einsum('gjts,sgd->gjtd', weights.astype(jnp.bfloat16), value_block, p...]
    pallas_call x0 -> x4, Pallas kernels: none -> 32.2 us  [the longest x1 17.3 us: experts(): pl.pallas_call(expert_kernel, in_specs=[pl.BlockSpec(memory_space=pltpu.S...]
    scatter x1 -> x0, local copies, waits for them, and re-layouts: 23 us -> none  [body(): jnp.zeros((EXPERTS * CAP, D), jnp.bfloat16).at[slot_index]]
  transfers between devices with their start and end apart: 7 -> 13, of which waited for: 6 -> 4; matrix products, arithmetic and copies ran while one was open for 3% -> 3% of each run, Pallas kernels for 0% -> 5%
where the time goes in v1:
time: 239 us; the launch traced here: 238 us
  blocking collectives  122 us (51%)
  starting transfers between devices  44.2 us (18%)
  Pallas kernels  32.2 us (13%)
  waiting for transfers between devices  14.9 us (6%)
  between operations  13.6 us (6%)
  local copies, waits for them, and re-layouts  6.45 us (3%)
  other arithmetic  4.09 us (2%)
    all_to_all x1, blocking collectives, body(): arrived = lax.all_to_all(outgoing, ('x', 'y'), 0, 0, tiled=True)  63.9 us
    all_to_all x1, blocking collectives, body(): back = lax.all_to_all(done, ('x', 'y'), 0, 0, tiled=True)  58.3 us
    ppermute x8, starting transfers between devices, spread(): lax.ppermute(source, ('x', 'c'), shifted(back, o))  19.7 us
    pallas_call x1, Pallas kernels, experts(): pl.pallas_call(expert_kernel, in_specs=[pl.BlockSpec(memory_space=pltpu.S...  17.3 us
    ppermute x1, starting transfers between devices, body(): packet_zh = lax.ppermute(packet, 'zh', swap)  16.3 us
    ppermute x8, waiting for transfers between devices, spread(): lax.ppermute(source, ('x', 'c'), shifted(back, o))  14.9 us
    pallas_call x1, Pallas kernels, attention(): pl.pallas_call(attention_kernel, in_specs=[pl.BlockSpec(memory_space=pltp...  10.8 us
    unnamed x11, local copies, waits for them, and re-layouts  5.39 us
  transfers between devices with their start and end apart: 13, of which 4 were waited for; matrix products, arithmetic and copies ran while one was open for 3% of the time, Pallas kernels for 5%

profile of v1, /device:TPU:1, one launch (start us, length us, event | category | flops | bytes accessed | tf_op | source)
XLA Modules:
  0.0 237.7 jit_solution(1787222826091368767)
XLA Ops:
  6.5 0.7 fusion.2
  7.3 0.9 fusion.1.rest_8_
  8.2 16.3 %collective-permute-start.1 = (bf16[144,512]{1,0:T(8,128)(2,1)S(1)}, bf16[144,512]{1,0:T(8,128)(2,1)S(1)}, u32[]{:S(2)}, u32[]{:S(2)}) collective-permute-start(bf16[144,512]{1,0:T(8,128)(2,1)S(1)} %fusion.1.rest_8_), channel_id=1, source_target_pairs={{0,64},{64,0},{1,65},{65,1},{2,66},{66,2},{3,67},{67,3},{4,68},{68... | collective-permute-start | bytes 442376 | tf_op jit(solution)/shard_map/ppermute | solution.py:311
  24.4 2.9 %collective-permute-start.2 = (bf16[144,512]{1,0:T(8,128)(2,1)S(1)}, bf16[144,512]{1,0:T(8,128)(2,1)S(1)}, u32[]{:S(2)}, u32[]{:S(2)}) collective-permute-start(bf16[144,512]{1,0:T(8,128)(2,1)S(1)} %fusion.1.rest_8_), channel_id=1, source_target_pairs={{0,32},{32,0},{1,33},{33,1},{2,34},{34,2},{3,35},{35,3},{4,36},{36... | collective-permute-start | bytes 442376 | tf_op jit(solution)/shard_map/ppermute | solution.py:306
  27.3 1.0 copy.29
  28.3 1.0 pad_maximum_fusion
  29.3 3.5 %collective-permute-start = (bf16[128,1152]{1,0:T(8,128)(2,1)S(1)}, bf16[128,1152]{1,0:T(8,128)(2,1)S(1)}, u32[]{:S(2)}, u32[]{:S(2)}) collective-permute-start(bf16[128,1152]{1,0:T(8,128)(2,1)S(1)} %pad_maximum_fusion), channel_id=1, source_target_pairs={{0,68},{1,101},{2,198},{3,231},{4,256},{5,289},{6,386},{7,419},{32... | collective-permute-start | bytes 884744 | tf_op jit(solution)/shard_map/ppermute | solution.py:314
  32.8 2.6 %collective-permute-start.3 = (bf16[144,512]{1,0:T(8,128)(2,1)S(1)}, bf16[144,512]{1,0:T(8,128)(2,1)S(1)}, u32[]{:S(2)}, u32[]{:S(2)}) collective-permute-start(bf16[144,512]{1,0:T(8,128)(2,1)S(1)} %fusion.1.rest_8_), channel_id=1, source_target_pairs={{0,128},{32,160},{128,256},{160,288},{256,384},{288,416},{1,129},{... | collective-permute-start | bytes 442376 | tf_op jit(solution)/shard_map/ppermute | solution.py:308
  35.4 2.2 collective-permute-start.4
  37.7 3.1 %collective-permute-start.5 = (bf16[144,512]{1,0:T(8,128)(2,1)S(1)}, bf16[144,512]{1,0:T(8,128)(2,1)S(1)}, u32[]{:S(2)}, u32[]{:S(2)}) collective-permute-start(bf16[144,512]{1,0:T(8,128)(2,1)S(1)} %fusion.1.rest_8_), channel_id=1, source_target_pairs={{0,256},{32,288},{128,384},{160,416},{1,257},{33,289},{129,385},{1... | collective-permute-start | bytes 442376 | tf_op jit(solution)/shard_map/ppermute | solution.py:308
  40.8 1.4 collective-permute-start.6
  42.2 0.8 collective-permute-done.4.rest_5_
  43.0 7.2 %collective-permute-done.5.rest_0_ = bf16[144,512]{1,0:T(8,128)(2,1)S(1)} collective-permute-done((bf16[144,512]{1,0:T(8,128)(2,1)S(1)}, bf16[144,512]{1,0:T(8,128)(2,1)S(1)}, u32[]{:S(2)}, u32[]{:S(2)}) %collective-permute-start.5) | collective-permute-done | bytes 147488 | tf_op jit(solution)/shard_map/ppermute | solution.py:308
  50.2 3.7 %collective-permute-done.6.rest_1_ = bf16[144,512]{1,0:T(8,128)(2,1)S(1)} collective-permute-done((bf16[144,512]{1,0:T(8,128)(2,1)S(1)}, bf16[144,512]{1,0:T(8,128)(2,1)S(1)}, u32[]{:S(2)}, u32[]{:S(2)}) %collective-permute-start.6) | collective-permute-done | bytes 147488 | tf_op jit(solution)/shard_map/ppermute | solution.py:308
  53.9 0.7 copy-done.3
  54.7 0.8 copy.25
  56.3 0.7 multiply_add_fusion
  57.1 5.7 %collective-permute-start.7 = (bf16[144,512]{1,0:T(8,128)(2,1)S(1)}, bf16[144,512]{1,0:T(8,128)(2,1)S(1)}, u32[]{:S(2)}, u32[]{:S(2)}) collective-permute-start(bf16[144,512]{1,0:T(8,128)(2,1)S(1)} %collective-permute-done.1.rest_10_), channel_id=1, source_target_pairs={{0,256},{32,288},{128,384},{160,416},{1,257},{33,289},{129,385},{1... | collective-permute-start | bytes 442376 | tf_op jit(solution)/shard_map/ppermute | solution.py:308
  62.8 1.5 collective-permute-start.8
  64.4 1.3 collective-permute-start.9
  65.7 1.9 collective-permute-start.10
  67.5 1.9 collective-permute-start.11
  70.3 0.8 copy.28
  71.1 0.9 slots.1
  72.1 3.1 %collective-permute-done.10.rest_7_ = bf16[144,512]{1,0:T(8,128)(2,1)S(1)} collective-permute-done((bf16[144,512]{1,0:T(8,128)(2,1)S(1)}, bf16[144,512]{1,0:T(8,128)(2,1)S(1)}, u32[]{:S(2)}, u32[]{:S(2)}) %collective-permute-start.10) | collective-permute-done | bytes 147488 | tf_op jit(solution)/shard_map/ppermute | solution.py:308
  75.2 1.0 copy-done.1
  76.3 1.0 copy-done.2
  77.3 10.8 %attend.1 = (f32[128,2048]{1,0:T(8,128)S(1)}, bf16[1152,2048]{1,0:T(8,128)(2,1)}) custom-call(s32[3]{0:T(128)S(1)} %pad_add_fusion.where_ref, bf16[128,2048]{1,0:T(8,128)(2,1)S(1)} %bitcast.24, f32[128,1]{1,0:T(8,128)S(1)} %copy.30.seg_ref, bf16[128,2048]{1,0:T(8,128)(2,1)S(1)} %bitcast.25, bf16[1,2048]{1,0:T(2,128)(2,1)S(1)} %broadcast_in_dim.7.gain_ref, ...), custom_call_target="tpu_custom_call" | custom-call | flops 1900000000 | bytes 9000000 | tf_op jit(solution)/shard_map/attend/pallas_call | solution.py:139
  88.1 63.9 %all_to_all.22 = bf16[16,72,2048]{2,1,0:T(8,128)(2,1)} all-to-all(bf16[16,72,2048]{2,1,0:T(8,128)(2,1)} %bitcast.26), channel_id=1, replica_groups=mesh['x'=4,'zh'=2,'c'=2,'y'=4,'zl'=8] {'x','y'}, dimensions={0} | all-to-all | bytes 9437184 | tf_op jit(solution)/shard_map/all_to_all | solution.py:329
  152.0 17.3 %expert_mlp.1 = bf16[1152,2048]{1,0:T(8,128)(2,1)} custom-call(s32[3]{0:T(128)} %copy-done, bf16[1152,2048]{1,0:T(8,128)(2,1)} %bitcast.27, bf16[4096,1152]{1,0:T(8,128)(2,1)} %all-gather.2.cloned.1.call-done.w_hbm), custom_call_target="tpu_custom_call" | custom-call | flops 6600000000 | bytes 19000000 | tf_op jit(solution)/shard_map/expert_mlp/pallas_call | solution.py:234
  169.4 58.3 %all_to_all.23 = bf16[16,72,2048]{2,1,0:T(8,128)(2,1)S(1)} all-to-all(bf16[16,72,2048]{2,1,0:T(8,128)(2,1)} %bitcast.28), channel_id=1, replica_groups=mesh['x'=4,'zh'=2,'c'=2,'y'=4,'zl'=8] {'x','y'}, dimensions={0} | all-to-all | bytes 9437184 | tf_op jit(solution)/shard_map/all_to_all | solution.py:331
  227.6 3.2 %combine.1 = bf16[128,2048]{1,0:T(8,128)(2,1)} custom-call(f32[128,2048]{1,0:T(8,128)S(1)} %get-tuple-element.26.hidden_ref, bf16[128,1152]{1,0:T(8,128)(2,1)S(1)} %get-tuple-element.27.high_ref, bf16[128,1152]{1,0:T(8,128)(2,1)S(1)} %get-tuple-element.28.low_ref, bf16[1152,2048]{1,0:T(8,128)(2,1)S(1)} %bitcast.22), custom_call_target="tpu_custom_call" | custom-call | flops 1200000000 | bytes 7000000 | tf_op jit(solution)/shard_map/combine/pallas_call | solution.py:264
  (25 shorter events, 1.9 us)
Async XLA Ops:
  6.5 145.5 %all-gather.2.cloned.1.call-start = ((), (), s32[]{:S(2)}) async-start(), calls=%async_computation.2 | async-start | bytes 9732096 | tf_op jit(solution)/shard_map/all_gather | solution.py:316
  8.2 29.5 %collective-permute-start.1 = (bf16[144,512]{1,0:T(8,128)(2,1)S(1)}, bf16[144,512]{1,0:T(8,128)(2,1)S(1)}, u32[]{:S(2)}, u32[]{:S(2)}) collective-permute-start(bf16[144,512]{1,0:T(8,128)(2,1)S(1)} %fusion.1.rest_8_), channel_id=1, source_target_pairs={{0,64},{64,0},{1,65},{65,1},{2,66},{66,2},{3,67},{67,3},{4,68},{68... | collective-permute-start | bytes 442376 | tf_op jit(solution)/shard_map/ppermute | solution.py:311
  24.4 16.3 %collective-permute-start.2 = (bf16[144,512]{1,0:T(8,128)(2,1)S(1)}, bf16[144,512]{1,0:T(8,128)(2,1)S(1)}, u32[]{:S(2)}, u32[]{:S(2)}) collective-permute-start(bf16[144,512]{1,0:T(8,128)(2,1)S(1)} %fusion.1.rest_8_), channel_id=1, source_target_pairs={{0,32},{32,0},{1,33},{33,1},{2,34},{34,2},{3,35},{35,3},{4,36},{36... | collective-permute-start | bytes 442376 | tf_op jit(solution)/shard_map/ppermute | solution.py:306
  29.3 24.6 %collective-permute-start = (bf16[128,1152]{1,0:T(8,128)(2,1)S(1)}, bf16[128,1152]{1,0:T(8,128)(2,1)S(1)}, u32[]{:S(2)}, u32[]{:S(2)}) collective-permute-start(bf16[128,1152]{1,0:T(8,128)(2,1)S(1)} %pad_maximum_fusion), channel_id=1, source_target_pairs={{0,68},{1,101},{2,198},{3,231},{4,256},{5,289},{6,386},{7,419},{32... | collective-permute-start | bytes 884744 | tf_op jit(solution)/shard_map/ppermute | solution.py:314
  32.8 9.4 %collective-permute-start.3 = (bf16[144,512]{1,0:T(8,128)(2,1)S(1)}, bf16[144,512]{1,0:T(8,128)(2,1)S(1)}, u32[]{:S(2)}, u32[]{:S(2)}) collective-permute-start(bf16[144,512]{1,0:T(8,128)(2,1)S(1)} %fusion.1.rest_8_), channel_id=1, source_target_pairs={{0,128},{32,160},{128,256},{160,288},{256,384},{288,416},{1,129},{... | collective-permute-start | bytes 442376 | tf_op jit(solution)/shard_map/ppermute | solution.py:308
  35.4 7.6 %collective-permute-start.4 = (bf16[144,512]{1,0:T(8,128)(2,1)S(1)}, bf16[144,512]{1,0:T(8,128)(2,1)S(1)}, u32[]{:S(2)}, u32[]{:S(2)}) collective-permute-start(bf16[144,512]{1,0:T(8,128)(2,1)S(1)} %fusion.1.rest_8_), channel_id=1, source_target_pairs={{0,160},{32,128},{128,288},{160,256},{256,416},{288,384},{1,161},{... | collective-permute-start | bytes 442376 | tf_op jit(solution)/shard_map/ppermute | solution.py:308
  37.7 12.5 %collective-permute-start.5 = (bf16[144,512]{1,0:T(8,128)(2,1)S(1)}, bf16[144,512]{1,0:T(8,128)(2,1)S(1)}, u32[]{:S(2)}, u32[]{:S(2)}) collective-permute-start(bf16[144,512]{1,0:T(8,128)(2,1)S(1)} %fusion.1.rest_8_), channel_id=1, source_target_pairs={{0,256},{32,288},{128,384},{160,416},{1,257},{33,289},{129,385},{1... | collective-permute-start | bytes 442376 | tf_op jit(solution)/shard_map/ppermute | solution.py:308
  40.8 13.2 %collective-permute-start.6 = (bf16[144,512]{1,0:T(8,128)(2,1)S(1)}, bf16[144,512]{1,0:T(8,128)(2,1)S(1)}, u32[]{:S(2)}, u32[]{:S(2)}) collective-permute-start(bf16[144,512]{1,0:T(8,128)(2,1)S(1)} %fusion.1.rest_8_), channel_id=1, source_target_pairs={{0,288},{32,256},{128,416},{160,384},{1,289},{33,257},{129,417},{1... | collective-permute-start | bytes 442376 | tf_op jit(solution)/shard_map/ppermute | solution.py:308
  53.9 0.7 copy-start.3
  57.1 14.9 %collective-permute-start.7 = (bf16[144,512]{1,0:T(8,128)(2,1)S(1)}, bf16[144,512]{1,0:T(8,128)(2,1)S(1)}, u32[]{:S(2)}, u32[]{:S(2)}) collective-permute-start(bf16[144,512]{1,0:T(8,128)(2,1)S(1)} %collective-permute-done.1.rest_10_), channel_id=1, source_target_pairs={{0,256},{32,288},{128,384},{160,416},{1,257},{33,289},{129,385},{1... | collective-permute-start | bytes 442376 | tf_op jit(solution)/shard_map/ppermute | solution.py:308
  62.8 9.2 %collective-permute-start.8 = (bf16[144,512]{1,0:T(8,128)(2,1)S(1)}, bf16[144,512]{1,0:T(8,128)(2,1)S(1)}, u32[]{:S(2)}, u32[]{:S(2)}) collective-permute-start(bf16[144,512]{1,0:T(8,128)(2,1)S(1)} %collective-permute-done.1.rest_10_), channel_id=1, source_target_pairs={{0,288},{32,256},{128,416},{160,384},{1,289},{33,257},{129,417},{1... | collective-permute-start | bytes 442376 | tf_op jit(solution)/shard_map/ppermute | solution.py:308
  64.4 7.7 %collective-permute-start.9 = (bf16[144,512]{1,0:T(8,128)(2,1)S(1)}, bf16[144,512]{1,0:T(8,128)(2,1)S(1)}, u32[]{:S(2)}, u32[]{:S(2)}) collective-permute-start(bf16[144,512]{1,0:T(8,128)(2,1)S(1)} %collective-permute-done.1.rest_10_), channel_id=1, source_target_pairs={{0,128},{32,160},{128,256},{160,288},{256,384},{288,416},{1,129},{... | collective-permute-start | bytes 442376 | tf_op jit(solution)/shard_map/ppermute | solution.py:308
  65.7 9.6 %collective-permute-start.10 = (bf16[144,512]{1,0:T(8,128)(2,1)S(1)}, bf16[144,512]{1,0:T(8,128)(2,1)S(1)}, u32[]{:S(2)}, u32[]{:S(2)}) collective-permute-start(bf16[144,512]{1,0:T(8,128)(2,1)S(1)} %collective-permute-done.1.rest_10_), channel_id=1, source_target_pairs={{0,160},{32,128},{128,288},{160,256},{256,416},{288,384},{1,161},{... | collective-permute-start | bytes 442376 | tf_op jit(solution)/shard_map/ppermute | solution.py:308
  67.5 7.7 %collective-permute-start.11 = (bf16[144,512]{1,0:T(8,128)(2,1)S(1)}, bf16[144,512]{1,0:T(8,128)(2,1)S(1)}, u32[]{:S(2)}, u32[]{:S(2)}) collective-permute-start(bf16[144,512]{1,0:T(8,128)(2,1)S(1)} %collective-permute-done.1.rest_10_), channel_id=1, source_target_pairs={{0,32},{32,0},{1,33},{33,1},{2,34},{34,2},{3,35},{35,3},{4,36},{36... | collective-permute-start | bytes 442376 | tf_op jit(solution)/shard_map/ppermute | solution.py:306
  72.1 79.9 %copy-start = (s32[3]{0:T(128)}, s32[3]{0:T(128)S(1)}, u32[]{:S(2)}) copy-start(s32[3]{0:T(128)S(1)} %pad_add_fusion.where_ref) | copy-start | bytes 40
  75.2 1.0 copy-start.1
  76.3 1.0 copy-start.2
Sparse Core Ops, SparseCore 0:
  54.8 78.6 all-gather.1

commit v2 on v1

v2 whole, which is shorter than its diff:
```python
import functools

import jax
import jax.numpy as jnp
from jax import lax
from jax.experimental import pallas as pl
from jax.experimental.pallas import tpu as pltpu
from jax.sharding import Mesh, PartitionSpec as P

D = 2048
HEADS = 16
KVH = 2
GROUPS = HEADS // KVH
HD = 128
FF = 384
EXPERTS = 32
TOPK = 8
TOK = 128
CAP = 36
SLOTS = EXPERTS * CAP
PACK = 144
WINDOW = 9
BLOCKS = 12
AXES = ("x", "zh", "c", "y", "zl")
F32 = jnp.float32
BF16 = jnp.bfloat16
NT = (((1,), (1,)), ((), ()))


def params(mib):
    return pltpu.CompilerParams(vmem_limit_bytes=mib * 1024 * 1024)


def slot_kernel(where_ref, ids_ref, gates_ref, send_ref, high_ref, low_ref):
    e = ids_ref[...]
    half = (e & 1) ^ (where_ref[3] & 1)
    ids = ((e >> 1) & 3) * 8 + (e >> 3) * 2 + half
    gates = gates_ref[...]
    line = lax.broadcasted_iota(jnp.int32, (EXPERTS, TOK), 0)
    named = jnp.zeros((EXPERTS, TOK), F32)
    gate = jnp.zeros((EXPERTS, TOK), F32)
    for k in range(TOPK):
        hit = ids[k : k + 1, :] == line
        named = named + jnp.where(hit, 1.0, 0.0)
        gate = gate + jnp.where(hit, gates[k : k + 1, :], 0.0)
    row = lax.broadcasted_iota(jnp.int32, (TOK, TOK), 0)
    earlier = (row < lax.broadcasted_iota(jnp.int32, (TOK, TOK), 1)).astype(F32).astype(BF16)
    rank = jnp.dot(named.astype(BF16), earlier, preferred_element_type=F32)
    rank = jnp.where(named > 0.0, rank, -1.0)
    slot = lax.broadcasted_iota(jnp.int32, (SLOTS, EXPERTS), 0).astype(F32)
    owner = jnp.floor((slot + 0.5) * (1.0 / CAP))
    place = slot - CAP * owner
    expert = lax.broadcasted_iota(jnp.int32, (SLOTS, EXPERTS), 1).astype(F32)
    spread = jnp.where(owner == expert, 1.0, 0.0).astype(BF16)
    rank_rows = jnp.dot(spread, rank.astype(BF16), preferred_element_type=F32)
    send_ref[...] = jnp.where(rank_rows == place[:, :1], 1.0, 0.0).astype(BF16)
    slot_t = lax.broadcasted_iota(jnp.int32, (1, SLOTS), 1).astype(F32)
    place_t = slot_t - CAP * jnp.floor((slot_t + 0.5) * (1.0 / CAP))
    rank_t = jnp.transpose(rank).astype(BF16)
    taken = lax.dot_general(rank_t, spread, NT, preferred_element_type=F32) == place_t
    gate = jnp.transpose(gate)
    high = gate.astype(BF16)
    low = (gate - high.astype(F32)).astype(BF16)
    for part, ref in ((high, high_ref), (low, low_ref)):
        wide = lax.dot_general(part, spread, NT, preferred_element_type=F32)
        ref[...] = jnp.where(taken, wide, 0.0).astype(BF16)


def slot_matrices(where, ids, gates):
    whole = pl.BlockSpec(memory_space=pltpu.VMEM)
    return pl.pallas_call(
        slot_kernel,
        in_specs=[pl.BlockSpec(memory_space=pltpu.SMEM)] + [whole] * 2,
        out_specs=(whole,) * 3,
        out_shape=(
            jax.ShapeDtypeStruct((SLOTS, TOK), BF16),
            jax.ShapeDtypeStruct((TOK, SLOTS), BF16),
            jax.ShapeDtypeStruct((TOK, SLOTS), BF16),
        ),
        compiler_params=params(16),
        cost_estimate=pl.CostEstimate(flops=40_000_000, bytes_accessed=1_000_000, transcendentals=0),
        name="slots",
    )(where, ids, gates)


def attention_kernel(where_ref, q_ref, seg_ref, res_ref, gain_ref, send_ref, *rest):
    blocks = rest[:BLOCKS]
    hidden_ref, out_ref, kv, segs, bias, hidden = rest[BLOCKS:]
    x, zh, c = where_ref[0], where_ref[1], where_ref[2]
    index = 0
    for back in (2, 1, 0):
        for other_zh in (0, 1):
            for other_c in (0, 1):
                zh_at = zh if other_zh == 0 else 1 - zh
                c_at = c if other_c == 0 else 1 - c
                slot = (2 - back) * 4 + zh_at * 2 + c_at
                kv[pl.ds(pl.multiple_of(slot * TOK, TOK), TOK), :] = blocks[index][:TOK, :]
                row = blocks[index][TOK:, :TOK].astype(F32)
                segs[pl.ds(slot, 1), :] = row[:1, :]
                index += 1
    first = zh * 2 + c
    own = x * 4 + first
    t = lax.broadcasted_iota(jnp.int32, (TOK, TOK), 0)
    s = lax.broadcasted_iota(jnp.int32, (TOK, TOK), 1)
    mine = jnp.sum(jnp.where(s == t, seg_ref[...].astype(F32), 0.0), axis=1, keepdims=True)
    for i in range(WINDOW):
        number = own - (WINDOW - 1) + i
        same = segs[pl.ds(first + i, 1), :] == mine
        allowed = same & (number >= 0)
        if i == WINDOW - 1:
            allowed = allowed & (s <= t)
        bias[:, i * TOK : (i + 1) * TOK] = jnp.where(allowed, 0.0, -1e30)
    start = pl.multiple_of(first * TOK, TOK)
    rate = HD ** (-0.5) * 1.4426950408889634
    for g in range(KVH):
        key = kv[pl.ds(start, WINDOW * TOK), g * HD : (g + 1) * HD]
        value = kv[pl.ds(start, WINDOW * TOK), (KVH + g) * HD : (KVH + g + 1) * HD]
        for j in range(GROUPS):
            columns = slice((g * GROUPS + j) * HD, (g * GROUPS + j + 1) * HD)
            score = lax.dot_general(q_ref[:, columns], key, NT, preferred_element_type=F32)
            score = score + bias[...]
            peak = jnp.max(score, axis=-1, keepdims=True)
            weight = jnp.exp2((score - peak) * rate)
            total = jnp.sum(weight, axis=-1, keepdims=True)
            mixed = jnp.dot(weight.astype(BF16), value, preferred_element_type=F32)
            hidden[:, columns] = res_ref[:, columns].astype(F32) + mixed / total
    full = hidden[...]
    hidden_ref[...] = full
    mean = jnp.mean(full * full, axis=-1, keepdims=True)
    normed = (full * lax.rsqrt(mean + 1e-6) * gain_ref[...].astype(F32)).astype(BF16)
    for n in range(0, D, 512):
        out_ref[:, n : n + 512] = jnp.dot(
            send_ref[...], normed[:, n : n + 512], preferred_element_type=F32
        ).astype(BF16)


def attention(where, q, seg, res, gain, send, blocks):
    whole = pl.BlockSpec(memory_space=pltpu.VMEM)
    return pl.pallas_call(
        attention_kernel,
        in_specs=[pl.BlockSpec(memory_space=pltpu.SMEM)] + [whole] * (5 + BLOCKS),
        out_specs=(whole, whole),
        out_shape=(
            jax.ShapeDtypeStruct((TOK, D), F32),
            jax.ShapeDtypeStruct((SLOTS, D), BF16),
        ),
        scratch_shapes=[
            pltpu.VMEM((BLOCKS * TOK, 2 * KVH * HD), BF16),
            pltpu.VMEM((16, TOK), F32),
            pltpu.VMEM((TOK, WINDOW * TOK), F32),
            pltpu.VMEM((TOK, D), F32),
        ],
        compiler_params=params(20),
        cost_estimate=pl.CostEstimate(
            flops=1_900_000_000, bytes_accessed=9_000_000, transcendentals=2_400_000
        ),
        name="attend",
    )(where, q, seg, res, gain, send, *blocks)


def slice_place(expert, x, zh, c):
    return (expert + 8 * zh + (x - 4 if c == 0 else 3 - x)) % 16


STEP = 576


def expert_kernel(where_ref, x_ref, w_hbm, out_ref, w_ref, down_ref, sem_w):
    x = where_ref[0]
    chunks = range(0, SLOTS, STEP)

    def source(which, k):
        place = slice_place(2 * x + which, k // 4, (k // 2) % 2, k % 2)
        return pl.ds(pl.multiple_of((which * 16 + place) * TOK, TOK), TOK)

    def weight_slice(which, k):
        return pltpu.make_async_copy(
            w_hbm.at[source(which, k)], w_ref.at[which, pl.ds(k * TOK, TOK)], sem_w.at[which, k]
        )

    def start(which, half):
        for k in range(half * 8, half * 8 + 8):
            weight_slice(which, k).start()

    def wait(which, half):
        for k in range(half * 8, half * 8 + 8):
            weight_slice(which, k).wait()

    start(0, 0)
    start(0, 1)

    def run(which, spans, first):
        def rows(columns):
            return jnp.concatenate([x_ref[a:b, columns] for a, b in spans], axis=0)

        gate_up = None
        if first:
            for half in (0, 1):
                wait(which, half)
                if which == 0:
                    start(1, half)
                for j in range(0, FF, TOK):
                    for k in range(half * 8, half * 8 + 8):
                        down_ref[which, j : j + TOK, k * TOK : (k + 1) * TOK] = w_ref[
                            which, k * TOK : (k + 1) * TOK, 2 * FF + j : 2 * FF + j + TOK
                        ]
                if which == 0:
                    part = slice(half * 1024, half * 1024 + 1024)
                    term = jnp.dot(
                        rows(part), w_ref[which, part, : 2 * FF], preferred_element_type=F32
                    )
                    gate_up = term if gate_up is None else gate_up + term
        if gate_up is None:
            gate_up = jnp.dot(
                rows(slice(0, D)), w_ref[which, :, : 2 * FF], preferred_element_type=F32
            )
        gate, up = gate_up[:, :FF], gate_up[:, FF:]
        near = 0.5 * gate
        inner = ((near + near * jnp.tanh(near)) * up).astype(BF16)
        return jnp.dot(inner, down_ref[which], preferred_element_type=F32).astype(BF16)

    line = lax.broadcasted_iota(jnp.int32, (16, 1), 0)
    for which in (0, 1):
        for i, chunk in enumerate(chunks):
            starts = range(chunk, chunk + STEP, 144)
            if which == 0:
                y = run(0, [(a + b, a + b + 48) for a in starts for b in (0, 96)], i == 0)
                for n, a in enumerate(starts):
                    out_ref[a : a + 48, :] = y[n * 96 : n * 96 + 48]
                    out_ref[a + 96 : a + 144, :] = y[n * 96 + 48 : n * 96 + 96]
            else:
                y = run(1, [(a + 32, a + 112) for a in starts], i == 0)
                for n, a in enumerate(starts):
                    p = y[n * 80 : n * 80 + 80]
                    head, tail = out_ref[a + 32 : a + 48, :], out_ref[a + 96 : a + 112, :]
                    out_ref[a + 32 : a + 48, :] = jnp.where(line < 4, head, p[:16])
                    out_ref[a + 48 : a + 96, :] = p[16:64]
                    out_ref[a + 96 : a + 112, :] = jnp.where(line < 12, p[64:], tail)


def experts(where, x, both):
    hbm = pl.BlockSpec(memory_space=pltpu.HBM)
    whole = pl.BlockSpec(memory_space=pltpu.VMEM)
    return pl.pallas_call(
        expert_kernel,
        in_specs=[pl.BlockSpec(memory_space=pltpu.SMEM), whole, hbm],
        out_specs=whole,
        out_shape=jax.ShapeDtypeStruct((SLOTS, D), BF16),
        scratch_shapes=[
            pltpu.VMEM((2, D, 3 * FF), BF16),
            pltpu.VMEM((2, FF, D), BF16),
            pltpu.SemaphoreType.DMA((2, 16)),
        ],
        compiler_params=params(44),
        cost_estimate=pl.CostEstimate(
            flops=6_600_000_000, bytes_accessed=19_000_000, transcendentals=540_000
        ),
        name="expert_mlp",
    )(where, x, both)


def combine_kernel(hidden_ref, high_ref, low_ref, back_ref, out_ref):
    back = back_ref[...]
    routed = jnp.dot(high_ref[...], back, preferred_element_type=F32)
    routed = routed + jnp.dot(low_ref[...], back, preferred_element_type=F32)
    out_ref[...] = (hidden_ref[...] + routed).astype(BF16)


def combine(hidden, high, low, back):
    wide = 512
    return pl.pallas_call(
        combine_kernel,
        grid=(D // wide,),
        in_specs=[
            pl.BlockSpec((TOK, wide), lambda i: (0, i)),
            pl.BlockSpec((TOK, SLOTS), lambda i: (0, 0)),
            pl.BlockSpec((TOK, SLOTS), lambda i: (0, 0)),
            pl.BlockSpec((SLOTS, wide), lambda i: (0, i)),
        ],
        out_specs=pl.BlockSpec((TOK, wide), lambda i: (0, i)),
        out_shape=jax.ShapeDtypeStruct((TOK, D), BF16),
        compiler_params=params(16),
        cost_estimate=pl.CostEstimate(
            flops=1_200_000_000, bytes_accessed=7_000_000, transcendentals=0
        ),
        name="combine",
    )(hidden, high, low, back)


def shifted(steps, swap):
    return [
        (x * 2 + c, (x + steps) * 2 + (c ^ swap)) for x in range(4) for c in range(2) if x + steps < 4
    ]


def to_expert_column():
    pairs = []
    for k in range(16):
        for zl in range(8):
            place = slice_place(zl, k // 4, (k // 2) % 2, k % 2)
            target = ((zl // 2 * 2 + place // 8) * 2 + zl % 2) * 8 + place % 8
            pairs.append((k * 8 + zl, target))
    return pairs


def body(q, k, v, seg, res, gain, ids, gates, w_gate, w_up, w_down):
    x, zh, c, y = (lax.axis_index(a) for a in ("x", "zh", "c", "y"))
    swap = [(0, 1), (1, 0)]

    seg_rows = jnp.pad(seg.astype(BF16), ((0, PACK - TOK - 1), (0, 2 * KVH * HD - TOK)))
    packet = jnp.concatenate([jnp.concatenate([k[0], v[0]], axis=1), seg_rows], axis=0)

    def spread(source):
        found = [[source, lax.ppermute(source, "c", swap)]]
        for back in (1, 2):
            found.append([lax.ppermute(source, ("x", "c"), shifted(back, o)) for o in (0, 1)])
        return found

    packet_zh = lax.ppermute(packet, "zh", swap)
    near = spread(packet)
    down = [w_down[0, j : j + TOK] for j in range(0, FF, TOK)]
    packed = jnp.concatenate([w_gate[0], w_up[0], *down], axis=1)
    packed, packet_zh, near = lax.optimization_barrier((packed, packet_zh, near))
    far = spread(packet_zh)
    packed = lax.ppermute(packed, ("x", "zh", "c", "zl"), to_expert_column())
    where = jnp.stack([x, zh, c, y]).astype(jnp.int32)
    ready = (*slot_matrices(where, ids[0].T, gates[0].T), gain[None], seg)
    packed, far, ready = lax.optimization_barrier((packed, far, ready))
    both = lax.all_gather(packed, ("c", "zh", "zl"), axis=0, tiled=True)
    blocks = [side[b][o] for b in (2, 1, 0) for side in (near, far) for o in (0, 1)]

    send, high, low, gain_row, seg_row = ready
    hidden, outgoing = attention(where, q[0], seg_row, res[0], gain_row, send, blocks)
    arrived = lax.all_to_all(outgoing, ("x", "y"), 0, 0, tiled=True)
    done = experts(where, arrived, both)
    back = lax.all_to_all(done, ("x", "y"), 0, 0, tiled=True)
    return combine(hidden, high, low, back)[None]


def solution(mesh):
    fine = Mesh(mesh.devices.reshape(4, 2, 2, 4, 8), AXES)
    exp, ctx = ("y", "zl"), ("x", "zh", "c")
    rows = P(exp, ctx, None)
    return jax.shard_map(
        body,
        mesh=fine,
        in_specs=(rows, rows, rows, P(exp, ctx), rows, P(), rows, rows, rows, rows, P(exp, None, ctx)),
        out_specs=rows,
        check_vma=False,
    )
```

time: 239 us -> 245 us (1.025)
  starting transfers between devices: 44.2 us -> 51.6 us
  local copies, waits for them, and re-layouts: 6.45 us -> 13.7 us
  Pallas kernels: 32.2 us -> 26 us
  blocking collectives: 122 us -> 125 us
  other arithmetic: 4.09 us -> 1.62 us
    ppermute x8, waiting for transfers between devices: 14.9 us -> 6.87 us  [spread(): lax.ppermute(source, ('x', 'c'), shifted(back, o))]
    unnamed x11 -> x22, local copies, waits for them, and re-layouts: 5.39 us -> 12.2 us
    ppermute x8, starting transfers between devices: 19.7 us -> 26.2 us  [spread(): lax.ppermute(source, ('x', 'c'), shifted(back, o))]
    all_gather x1, waiting for transfers between devices: 0.01 us -> 5.63 us  [body(): both = lax.all_gather(packed, ('c', 'zh', 'zl'), axis=0, tiled=True)]
    pallas_call x1, Pallas kernels: 17.3 us -> 13.1 us  [experts(): pl.pallas_call(expert_kernel, in_specs=[pl.BlockSpec(memory_space=pltpu.S...]
    all_to_all x1, blocking collectives: 58.3 us -> 61.9 us  [body(): back = lax.all_to_all(done, ('x', 'y'), 0, 0, tiled=True)]
  transfers between devices with their start and end apart: 13 -> 13, of which waited for: 4 -> 4; matrix products, arithmetic and copies ran while one was open for 3% -> 2% of each run, Pallas kernels for 5% -> 4%
where the time goes in v2:
time: 245 us; the launch traced here: 244 us
  blocking collectives  125 us (51%)
  starting transfers between devices  51.6 us (21%)
  Pallas kernels  26 us (11%)
  local copies, waits for them, and re-layouts  13.7 us (6%)
  between operations  13.6 us (6%)
  waiting for transfers between devices  12.5 us (5%)
    all_to_all x1, blocking collectives, body(): arrived = lax.all_to_all(outgoing, ('x', 'y'), 0, 0, tiled=True)  62.9 us
    all_to_all x1, blocking collectives, body(): back = lax.all_to_all(done, ('x', 'y'), 0, 0, tiled=True)  61.9 us
    ppermute x8, starting transfers between devices, spread(): lax.ppermute(source, ('x', 'c'), shifted(back, o))  26.2 us
    ppermute x1, starting transfers between devices, body(): packet_zh = lax.ppermute(packet, 'zh', swap)  16.3 us
    pallas_call x1, Pallas kernels, experts(): pl.pallas_call(expert_kernel, in_specs=[pl.BlockSpec(memory_space=pltpu.S...  13.1 us
    unnamed x22, local copies, waits for them, and re-layouts  12.2 us
    pallas_call x1, Pallas kernels, attention(): pl.pallas_call(attention_kernel, in_specs=[pl.BlockSpec(memory_space=pltp...  8.56 us
    ppermute x8, waiting for transfers between devices, spread(): lax.ppermute(source, ('x', 'c'), shifted(back, o))  6.87 us
  transfers between devices with their start and end apart: 13, of which 4 were waited for; matrix products, arithmetic and copies ran while one was open for 2% of the time, Pallas kernels for 4%

profile of v2, /device:TPU:1, one launch (start us, length us, event | category | flops | bytes accessed | tf_op | source)
XLA Modules:
  0.0 243.8 jit_solution(7437497608638457622)
XLA Ops:
  7.2 0.9 fusion.1.rest_8_
  8.1 16.3 %collective-permute-start = (bf16[144,512]{1,0:T(8,128)(2,1)S(1)}, bf16[144,512]{1,0:T(8,128)(2,1)S(1)}, u32[]{:S(2)}, u32[]{:S(2)}) collective-permute-start(bf16[144,512]{1,0:T(8,128)(2,1)S(1)} %fusion.1.rest_8_), channel_id=1, source_target_pairs={{0,64},{64,0},{1,65},{65,1},{2,66},{66,2},{3,67},{67,3},{4,68},{68... | collective-permute-start | bytes 442376 | tf_op jit(solution)/shard_map/ppermute | solution.py:319
  24.4 2.9 %collective-permute-start.1 = (bf16[144,512]{1,0:T(8,128)(2,1)S(1)}, bf16[144,512]{1,0:T(8,128)(2,1)S(1)}, u32[]{:S(2)}, u32[]{:S(2)}) collective-permute-start(bf16[144,512]{1,0:T(8,128)(2,1)S(1)} %fusion.1.rest_8_), channel_id=1, source_target_pairs={{0,32},{32,0},{1,33},{33,1},{2,34},{34,2},{3,35},{35,3},{4,36},{36... | collective-permute-start | bytes 442376 | tf_op jit(solution)/shard_map/ppermute | solution.py:314
  27.2 3.1 %collective-permute-start.2 = (bf16[144,512]{1,0:T(8,128)(2,1)S(1)}, bf16[144,512]{1,0:T(8,128)(2,1)S(1)}, u32[]{:S(2)}, u32[]{:S(2)}) collective-permute-start(bf16[144,512]{1,0:T(8,128)(2,1)S(1)} %fusion.1.rest_8_), channel_id=1, source_target_pairs={{0,128},{32,160},{128,256},{160,288},{256,384},{288,416},{1,129},{... | collective-permute-start | bytes 442376 | tf_op jit(solution)/shard_map/ppermute | solution.py:316
  30.4 3.3 %collective-permute-start.3 = (bf16[144,512]{1,0:T(8,128)(2,1)S(1)}, bf16[144,512]{1,0:T(8,128)(2,1)S(1)}, u32[]{:S(2)}, u32[]{:S(2)}) collective-permute-start(bf16[144,512]{1,0:T(8,128)(2,1)S(1)} %fusion.1.rest_8_), channel_id=1, source_target_pairs={{0,160},{32,128},{128,288},{160,256},{256,416},{288,384},{1,161},{... | collective-permute-start | bytes 442376 | tf_op jit(solution)/shard_map/ppermute | solution.py:316
  33.7 3.0 %collective-permute-start.4 = (bf16[144,512]{1,0:T(8,128)(2,1)S(1)}, bf16[144,512]{1,0:T(8,128)(2,1)S(1)}, u32[]{:S(2)}, u32[]{:S(2)}) collective-permute-start(bf16[144,512]{1,0:T(8,128)(2,1)S(1)} %fusion.1.rest_8_), channel_id=1, source_target_pairs={{0,256},{32,288},{128,384},{160,416},{1,257},{33,289},{129,385},{1... | collective-permute-start | bytes 442376 | tf_op jit(solution)/shard_map/ppermute | solution.py:316
  36.7 0.9 bitcast_dynamic-update-slice_fusion.1
  37.6 0.9 bitcast_dynamic-update-slice_fusion
  38.5 0.8 bitcast_dynamic-update-slice_fusion.4
  39.3 0.8 bitcast_dynamic-update-slice_fusion.3
  40.0 1.5 collective-permute-start.5
  41.5 0.8 bitcast_dynamic-update-slice_fusion.2
  42.3 2.3 collective-permute-done.5.rest_1_
  44.6 2.8 %collective-permute-start.7 = (bf16[144,512]{1,0:T(8,128)(2,1)S(1)}, bf16[144,512]{1,0:T(8,128)(2,1)S(1)}, u32[]{:S(2)}, u32[]{:S(2)}) collective-permute-start(bf16[144,512]{1,0:T(8,128)(2,1)S(1)} %collective-permute-done.rest_10_), channel_id=1, source_target_pairs={{0,32},{32,0},{1,33},{33,1},{2,34},{34,2},{3,35},{35,3},{4,36},{36... | collective-permute-start | bytes 442376 | tf_op jit(solution)/shard_map/ppermute | solution.py:314
  47.4 3.5 %collective-permute-start.6 = (bf16[128,1152]{1,0:T(8,128)(2,1)S(1)}, bf16[128,1152]{1,0:T(8,128)(2,1)S(1)}, u32[]{:S(2)}, u32[]{:S(2)}) collective-permute-start(bf16[128,1152]{1,0:T(8,128)(2,1)S(1)} %bitcast_dynamic-update-slice_fusion.2), channel_id=1, source_target_pairs={{0,68},{1,101},{2,198},{3,231},{4,256},{5,289},{6,386},{7,419},{32... | collective-permute-start | bytes 884744 | tf_op jit(solution)/shard_map/ppermute | solution.py:325
  50.9 2.6 %collective-permute-start.8 = (bf16[144,512]{1,0:T(8,128)(2,1)S(1)}, bf16[144,512]{1,0:T(8,128)(2,1)S(1)}, u32[]{:S(2)}, u32[]{:S(2)}) collective-permute-start(bf16[144,512]{1,0:T(8,128)(2,1)S(1)} %collective-permute-done.rest_10_), channel_id=1, source_target_pairs={{0,128},{32,160},{128,256},{160,288},{256,384},{288,416},{1,129},{... | collective-permute-start | bytes 442376 | tf_op jit(solution)/shard_map/ppermute | solution.py:316
  53.6 9.5 %collective-permute-start.9 = (bf16[144,512]{1,0:T(8,128)(2,1)S(1)}, bf16[144,512]{1,0:T(8,128)(2,1)S(1)}, u32[]{:S(2)}, u32[]{:S(2)}) collective-permute-start(bf16[144,512]{1,0:T(8,128)(2,1)S(1)} %collective-permute-done.rest_10_), channel_id=1, source_target_pairs={{0,160},{32,128},{128,288},{160,256},{256,416},{288,384},{1,161},{... | collective-permute-start | bytes 442376 | tf_op jit(solution)/shard_map/ppermute | solution.py:316
  63.0 1.3 collective-permute-start.10
  64.3 2.0 collective-permute-start.11
  68.5 1.2 slots.1
  70.4 1.4 collective-permute-done.10.rest_2_
  71.8 3.2 %collective-permute-done.11.rest_3_ = bf16[144,512]{1,0:T(8,128)(2,1)S(1)} collective-permute-done((bf16[144,512]{1,0:T(8,128)(2,1)S(1)}, bf16[144,512]{1,0:T(8,128)(2,1)S(1)}, u32[]{:S(2)}, u32[]{:S(2)}) %collective-permute-start.11) | collective-permute-done | bytes 147488 | tf_op jit(solution)/shard_map/ppermute | solution.py:316
  75.7 1.0 copy-done.1
  76.7 1.0 copy-done.2
  78.4 1.0 copy-done.7
  79.4 8.6 %attend.1 = (f32[128,2048]{1,0:T(8,128)S(1)}, bf16[1152,2048]{1,0:T(8,128)(2,1)S(1)}) custom-call(s32[4]{0:T(128)S(1)} %pad_add_fusion.where_ref, bf16[128,2048]{1,0:T(8,128)(2,1)S(1)} %bitcast.33, s32[1,128]{1,0:T(1,128)S(1)} %copy-done.5, bf16[128,2048]{1,0:T(8,128)(2,1)S(1)} %bitcast.34, bf16[1,2048]{1,0:T(2,128)(2,1)S(1)} %broadcast_in_dim.6.gain_ref, ...), custom_call_target="tpu_custom_call" | custom-call | flops 1900000000 | bytes 9000000 | tf_op jit(solution)/shard_map/attend/pallas_call | solution.py:139
  88.0 62.9 %all_to_all.22 = bf16[16,72,2048]{2,1,0:T(8,128)(2,1)} all-to-all(bf16[16,72,2048]{2,1,0:T(8,128)(2,1)S(1)} %bitcast.30), channel_id=1, replica_groups=mesh['x'=4,'zh'=2,'c'=2,'y'=4,'zl'=8] {'x','y'}, dimensions={0} | all-to-all | bytes 9437184 | tf_op jit(solution)/shard_map/all_to_all | solution.py:334
  150.9 5.6 %all-gather.2.cloned.1.call-done.w_hbm = bf16[4096,1152]{1,0:T(8,128)(2,1)} async-done(((bf16[128,1152]{1,0:T(8,128)(2,1)}), bf16[4096,1152]{1,0:T(8,128)(2,1)}) %all-gather.2.cloned.1.call-update) | async-done | bytes 9437200 | tf_op jit(solution)/shard_map/all_gather | solution.py:329
  156.5 2.3 copy-done
  158.8 13.1 %expert_mlp.1 = bf16[1152,2048]{1,0:T(8,128)(2,1)S(1)} custom-call(s32[4]{0:T(128)S(1)} %pad_add_fusion.where_ref, bf16[1152,2048]{1,0:T(8,128)(2,1)S(1)} %bitcast.31, bf16[4096,1152]{1,0:T(8,128)(2,1)} %all-gather.2.cloned.1.call-done.w_hbm), custom_call_target="tpu_custom_call" | custom-call | flops 6600000000 | bytes 19000000 | tf_op jit(solution)/shard_map/expert_mlp/pallas_call | solution.py:244
  171.9 61.9 %all_to_all.23 = bf16[16,72,2048]{2,1,0:T(8,128)(2,1)S(1)} all-to-all(bf16[16,72,2048]{2,1,0:T(8,128)(2,1)S(1)} %bitcast.32), channel_id=1, replica_groups=mesh['x'=4,'zh'=2,'c'=2,'y'=4,'zl'=8] {'x','y'}, dimensions={0} | all-to-all | bytes 9437184 | tf_op jit(solution)/shard_map/all_to_all | solution.py:336
  233.8 3.2 %combine.1 = bf16[128,2048]{1,0:T(8,128)(2,1)} custom-call(f32[128,2048]{1,0:T(8,128)S(1)} %get-tuple-element.50.hidden_ref, bf16[128,1152]{1,0:T(8,128)(2,1)S(1)} %get-tuple-element.51.high_ref, bf16[128,1152]{1,0:T(8,128)(2,1)S(1)} %get-tuple-element.52.low_ref, bf16[1152,2048]{1,0:T(8,128)(2,1)S(1)} %bitcast.29), custom_call_target="tpu_custom_call" | custom-call | flops 1200000000 | bytes 7000000 | tf_op jit(solution)/shard_map/combine/pallas_call | solution.py:271
  (28 shorter events, 4.9 us)
Async XLA Ops:
  6.5 150.0 %all-gather.2.cloned.1.call-start = ((), (), s32[]{:S(2)}) async-start(), calls=%async_computation.2 | async-start | bytes 9732096 | tf_op jit(solution)/shard_map/all_gather | solution.py:329
  8.1 31.9 %collective-permute-start = (bf16[144,512]{1,0:T(8,128)(2,1)S(1)}, bf16[144,512]{1,0:T(8,128)(2,1)S(1)}, u32[]{:S(2)}, u32[]{:S(2)}) collective-permute-start(bf16[144,512]{1,0:T(8,128)(2,1)S(1)} %fusion.1.rest_8_), channel_id=1, source_target_pairs={{0,64},{64,0},{1,65},{65,1},{2,66},{66,2},{3,67},{67,3},{4,68},{68... | collective-permute-start | bytes 442376 | tf_op jit(solution)/shard_map/ppermute | solution.py:319
  24.4 17.9 %collective-permute-start.1 = (bf16[144,512]{1,0:T(8,128)(2,1)S(1)}, bf16[144,512]{1,0:T(8,128)(2,1)S(1)}, u32[]{:S(2)}, u32[]{:S(2)}) collective-permute-start(bf16[144,512]{1,0:T(8,128)(2,1)S(1)} %fusion.1.rest_8_), channel_id=1, source_target_pairs={{0,32},{32,0},{1,33},{33,1},{2,34},{34,2},{3,35},{35,3},{4,36},{36... | collective-permute-start | bytes 442376 | tf_op jit(solution)/shard_map/ppermute | solution.py:314
  27.2 15.1 %collective-permute-start.2 = (bf16[144,512]{1,0:T(8,128)(2,1)S(1)}, bf16[144,512]{1,0:T(8,128)(2,1)S(1)}, u32[]{:S(2)}, u32[]{:S(2)}) collective-permute-start(bf16[144,512]{1,0:T(8,128)(2,1)S(1)} %fusion.1.rest_8_), channel_id=1, source_target_pairs={{0,128},{32,160},{128,256},{160,288},{256,384},{288,416},{1,129},{... | collective-permute-start | bytes 442376 | tf_op jit(solution)/shard_map/ppermute | solution.py:316
  30.4 11.9 %collective-permute-start.3 = (bf16[144,512]{1,0:T(8,128)(2,1)S(1)}, bf16[144,512]{1,0:T(8,128)(2,1)S(1)}, u32[]{:S(2)}, u32[]{:S(2)}) collective-permute-start(bf16[144,512]{1,0:T(8,128)(2,1)S(1)} %fusion.1.rest_8_), channel_id=1, source_target_pairs={{0,160},{32,128},{128,288},{160,256},{256,416},{288,384},{1,161},{... | collective-permute-start | bytes 442376 | tf_op jit(solution)/shard_map/ppermute | solution.py:316
  33.7 8.6 %collective-permute-start.4 = (bf16[144,512]{1,0:T(8,128)(2,1)S(1)}, bf16[144,512]{1,0:T(8,128)(2,1)S(1)}, u32[]{:S(2)}, u32[]{:S(2)}) collective-permute-start(bf16[144,512]{1,0:T(8,128)(2,1)S(1)} %fusion.1.rest_8_), channel_id=1, source_target_pairs={{0,256},{32,288},{128,384},{160,416},{1,257},{33,289},{129,385},{1... | collective-permute-start | bytes 442376 | tf_op jit(solution)/shard_map/ppermute | solution.py:316
  40.0 4.6 %collective-permute-start.5 = (bf16[144,512]{1,0:T(8,128)(2,1)S(1)}, bf16[144,512]{1,0:T(8,128)(2,1)S(1)}, u32[]{:S(2)}, u32[]{:S(2)}) collective-permute-start(bf16[144,512]{1,0:T(8,128)(2,1)S(1)} %fusion.1.rest_8_), channel_id=1, source_target_pairs={{0,288},{32,256},{128,416},{160,384},{1,289},{33,257},{129,417},{1... | collective-permute-start | bytes 442376 | tf_op jit(solution)/shard_map/ppermute | solution.py:316
  44.6 19.7 %collective-permute-start.7 = (bf16[144,512]{1,0:T(8,128)(2,1)S(1)}, bf16[144,512]{1,0:T(8,128)(2,1)S(1)}, u32[]{:S(2)}, u32[]{:S(2)}) collective-permute-start(bf16[144,512]{1,0:T(8,128)(2,1)S(1)} %collective-permute-done.rest_10_), channel_id=1, source_target_pairs={{0,32},{32,0},{1,33},{33,1},{2,34},{34,2},{3,35},{35,3},{4,36},{36... | collective-permute-start | bytes 442376 | tf_op jit(solution)/shard_map/ppermute | solution.py:314
  47.4 27.5 %collective-permute-start.6 = (bf16[128,1152]{1,0:T(8,128)(2,1)S(1)}, bf16[128,1152]{1,0:T(8,128)(2,1)S(1)}, u32[]{:S(2)}, u32[]{:S(2)}) collective-permute-start(bf16[128,1152]{1,0:T(8,128)(2,1)S(1)} %bitcast_dynamic-update-slice_fusion.2), channel_id=1, source_target_pairs={{0,68},{1,101},{2,198},{3,231},{4,256},{5,289},{6,386},{7,419},{32... | collective-permute-start | bytes 884744 | tf_op jit(solution)/shard_map/ppermute | solution.py:325
  50.9 19.5 %collective-permute-start.8 = (bf16[144,512]{1,0:T(8,128)(2,1)S(1)}, bf16[144,512]{1,0:T(8,128)(2,1)S(1)}, u32[]{:S(2)}, u32[]{:S(2)}) collective-permute-start(bf16[144,512]{1,0:T(8,128)(2,1)S(1)} %collective-permute-done.rest_10_), channel_id=1, source_target_pairs={{0,128},{32,160},{128,256},{160,288},{256,384},{288,416},{1,129},{... | collective-permute-start | bytes 442376 | tf_op jit(solution)/shard_map/ppermute | solution.py:316
  53.6 16.8 %collective-permute-start.9 = (bf16[144,512]{1,0:T(8,128)(2,1)S(1)}, bf16[144,512]{1,0:T(8,128)(2,1)S(1)}, u32[]{:S(2)}, u32[]{:S(2)}) collective-permute-start(bf16[144,512]{1,0:T(8,128)(2,1)S(1)} %collective-permute-done.rest_10_), channel_id=1, source_target_pairs={{0,160},{32,128},{128,288},{160,256},{256,416},{288,384},{1,161},{... | collective-permute-start | bytes 442376 | tf_op jit(solution)/shard_map/ppermute | solution.py:316
  63.0 8.7 %collective-permute-start.10 = (bf16[144,512]{1,0:T(8,128)(2,1)S(1)}, bf16[144,512]{1,0:T(8,128)(2,1)S(1)}, u32[]{:S(2)}, u32[]{:S(2)}) collective-permute-start(bf16[144,512]{1,0:T(8,128)(2,1)S(1)} %collective-permute-done.rest_10_), channel_id=1, source_target_pairs={{0,256},{32,288},{128,384},{160,416},{1,257},{33,289},{129,385},{1... | collective-permute-start | bytes 442376 | tf_op jit(solution)/shard_map/ppermute | solution.py:316
  64.3 10.6 %collective-permute-start.11 = (bf16[144,512]{1,0:T(8,128)(2,1)S(1)}, bf16[144,512]{1,0:T(8,128)(2,1)S(1)}, u32[]{:S(2)}, u32[]{:S(2)}) collective-permute-start(bf16[144,512]{1,0:T(8,128)(2,1)S(1)} %collective-permute-done.rest_10_), channel_id=1, source_target_pairs={{0,288},{32,256},{128,416},{160,384},{1,289},{33,257},{129,417},{1... | collective-permute-start | bytes 442376 | tf_op jit(solution)/shard_map/ppermute | solution.py:316
  67.1 0.7 copy-start.3
  67.8 0.7 copy-start.4
  69.7 0.7 copy-start.6
  74.9 0.7 copy-start.8
  75.7 1.0 copy-start.1
  76.7 1.0 copy-start.2
  77.8 0.7 copy-start.5
  78.4 1.0 copy-start.7
  156.5 2.3 copy-start
Sparse Core Ops, SparseCore 0:
  75.8 80.6 all-gather.1

commit v3 on v2

--- a/solution.py
+++ b/solution.py
@@ -29,6 +29,43 @@
 
 def params(mib):
     return pltpu.CompilerParams(vmem_limit_bytes=mib * 1024 * 1024)
+
+
+def pack_kernel(k_in, v_in, gate_in, up_in, down_in, seg_ref, packet_ref, packed_ref, sem):
+    pieces = [
+        (gate_in, packed_ref.at[:, pl.ds(0, FF)]),
+        (up_in, packed_ref.at[:, pl.ds(FF, FF)]),
+        (k_in, packet_ref.at[pl.ds(0, TOK), pl.ds(0, KVH * HD)]),
+        (v_in, packet_ref.at[pl.ds(0, TOK), pl.ds(KVH * HD, KVH * HD)]),
+    ]
+    for j in range(0, FF, TOK):
+        pieces.append((down_in.at[pl.ds(j, TOK)], packed_ref.at[:, pl.ds(2 * FF + j, TOK)]))
+    copies = [pltpu.make_async_copy(a, b, sem.at[n]) for n, (a, b) in enumerate(pieces)]
+    for copy in copies:
+        copy.start()
+    line = lax.broadcasted_iota(jnp.int32, (PACK - TOK, TOK), 0)
+    row = jnp.where(line == 0, seg_ref[...].astype(F32), 0.0)
+    packet_ref[TOK:, :TOK] = row.astype(BF16)
+    packet_ref[TOK:, TOK:] = jnp.zeros((PACK - TOK, 2 * KVH * HD - TOK), BF16)
+    for copy in copies:
+        copy.wait()
+
+
+def pack(k, v, w_gate, w_up, w_down, seg):
+    whole = pl.BlockSpec(memory_space=pltpu.VMEM)
+    return pl.pallas_call(
+        pack_kernel,
+        in_specs=[pl.BlockSpec(memory_space=pl.ANY)] * 5 + [whole],
+        out_specs=(whole, whole),
+        out_shape=(
+            jax.ShapeDtypeStruct((PACK, 2 * KVH * HD), BF16),
+            jax.ShapeDtypeStruct((TOK, 3 * FF), BF16),
+        ),
+        scratch_shapes=[pltpu.SemaphoreType.DMA((4 + FF // TOK,))],
+        compiler_params=params(56),
+        cost_estimate=pl.CostEstimate(flops=0, bytes_accessed=1_000_000, transcendentals=0),
+        name="pack",
+    )(k, v, w_gate, w_up, w_down, seg)
 
 
 def slot_kernel(where_ref, ids_ref, gates_ref, send_ref, high_ref, low_ref):
@@ -307,8 +344,8 @@
     x, zh, c, y = (lax.axis_index(a) for a in ("x", "zh", "c", "y"))
     swap = [(0, 1), (1, 0)]
 
-    seg_rows = jnp.pad(seg.astype(BF16), ((0, PACK - TOK - 1), (0, 2 * KVH * HD - TOK)))
-    packet = jnp.concatenate([jnp.concatenate([k[0], v[0]], axis=1), seg_rows], axis=0)
+    packet, packed = pack(k[0], v[0], w_gate[0], w_up[0], w_down[0], seg)
+    packed = lax.ppermute(packed, ("x", "zh", "c", "zl"), to_expert_column())
 
     def spread(source):
         found = [[source, lax.ppermute(source, "c", swap)]]
@@ -317,16 +354,14 @@
         return found
 
     packet_zh = lax.ppermute(packet, "zh", swap)
-    near = spread(packet)
-    down = [w_down[0, j : j + TOK] for j in range(0, FF, TOK)]
-    packed = jnp.concatenate([w_gate[0], w_up[0], *down], axis=1)
+    packed, packet_near = lax.optimization_barrier((packed, packet))
+    near = spread(packet_near)
     packed, packet_zh, near = lax.optimization_barrier((packed, packet_zh, near))
+    both = lax.all_gather(packed, ("c", "zh", "zl"), axis=0, tiled=True)
     far = spread(packet_zh)
-    packed = lax.ppermute(packed, ("x", "zh", "c", "zl"), to_expert_column())
     where = jnp.stack([x, zh, c, y]).astype(jnp.int32)
     ready = (*slot_matrices(where, ids[0].T, gates[0].T), gain[None], seg)
-    packed, far, ready = lax.optimization_barrier((packed, far, ready))
-    both = lax.all_gather(packed, ("c", "zh", "zl"), axis=0, tiled=True)
+    far, ready = lax.optimization_barrier((far, ready))
     blocks = [side[b][o] for b in (2, 1, 0) for side in (near, far) for o in (0, 1)]
 
     send, high, low, gain_row, seg_row = ready

time: 245 us -> 247 us (level)
  starting transfers between devices: 51.6 us -> 61.9 us
  local copies, waits for them, and re-layouts: 13.7 us -> 8.06 us
  blocking collectives: 125 us -> 121 us
    ppermute x2, starting transfers between devices: 5.67 us -> 24.8 us  [spread(): found = [[source, lax.ppermute(source, 'c', swap)]]]
    ppermute x8, starting transfers between devices: 26.2 us -> 16.7 us  [spread(): lax.ppermute(source, ('x', 'c'), shifted(back, o))]
    all_gather x1, waiting for transfers between devices: 5.63 us -> 0.01 us  [body(): both = lax.all_gather(packed, ('c', 'zh', 'zl'), axis=0, tiled=True)]
    unnamed x22 -> x16, local copies, waits for them, and re-layouts: 12.2 us -> 7.37 us
    ppermute x8, waiting for transfers between devices: 6.87 us -> 11.3 us  [spread(): lax.ppermute(source, ('x', 'c'), shifted(back, o))]
    all_to_all x1, blocking collectives: 61.9 us -> 57.7 us  [body(): back = lax.all_to_all(done, ('x', 'y'), 0, 0, tiled=True)]
    ppermute x1, starting transfers between devices: 3.45 us -> 7.64 us  [body(): packed = lax.ppermute(packed, ('x', 'zh', 'c', 'zl'), to_expert_column())]
    ppermute x1, starting transfers between devices: 16.3 us -> 12.7 us  [body(): packet_zh = lax.ppermute(packet, 'zh', swap)]
  transfers between devices with their start and end apart: 13 -> 13, of which waited for: 4 -> 4; matrix products, arithmetic and copies ran while one was open for 2% -> 0% of each run, Pallas kernels for 4% -> 4%
where the time goes in v3:
time: 247 us; the launch traced here: 244 us
  blocking collectives  121 us (49%)
  starting transfers between devices  61.9 us (25%)
  Pallas kernels  28.4 us (11%)
  between operations  13.6 us (6%)
  waiting for transfers between devices  11.3 us (5%)
  local copies, waits for them, and re-layouts  8.06 us (3%)
    all_to_all x1, blocking collectives, body(): arrived = lax.all_to_all(outgoing, ('x', 'y'), 0, 0, tiled=True)  62.9 us
    all_to_all x1, blocking collectives, body(): back = lax.all_to_all(done, ('x', 'y'), 0, 0, tiled=True)  57.7 us
    ppermute x2, starting transfers between devices, spread(): found = [[source, lax.ppermute(source, 'c', swap)]]  24.8 us
    ppermute x8, starting transfers between devices, spread(): lax.ppermute(source, ('x', 'c'), shifted(back, o))  16.7 us
    pallas_call x1, Pallas kernels, experts(): pl.pallas_call(expert_kernel, in_specs=[pl.BlockSpec(memory_space=pltpu.S...  13.1 us
    ppermute x1, starting transfers between devices, body(): packet_zh = lax.ppermute(packet, 'zh', swap)  12.7 us
    ppermute x8, waiting for transfers between devices, spread(): lax.ppermute(source, ('x', 'c'), shifted(back, o))  11.3 us
    pallas_call x1, Pallas kernels, attention(): pl.pallas_call(attention_kernel, in_specs=[pl.BlockSpec(memory_space=pltp...  8.53 us
  transfers between devices with their start and end apart: 13, of which 4 were waited for; matrix products, arithmetic and copies ran while one was open for 0% of the time, Pallas kernels for 4%

profile of v3, /device:TPU:1, one launch (start us, length us, event | category | flops | bytes accessed | tf_op | source)
XLA Modules:
  0.0 244.0 jit_solution(12383226162800807971)
XLA Ops:
  6.5 2.4 %pack.1 = (bf16[144,512]{1,0:T(8,128)(2,1)}, bf16[128,1152]{1,0:T(8,128)(2,1)}) custom-call(bf16[128,256]{1,0:T(8,128)(2,1)} %bitcast.33, bf16[128,256]{1,0:T(8,128)(2,1)} %bitcast.34, bf16[128,384]{1,0:T(8,128)(2,1)} %bitcast.30, bf16[128,384]{1,0:T(8,128)(2,1)} %bitcast.31, bf16[384,128]{1,0:T(8,128)(2,1)} %bitcast.32, s32[1,128]{1,0:T(1,128)} %seg_ref.2), custom_call_target="tpu_custom_call" | custom-call | bytes 1000000 | tf_op jit(solution)/shard_map/pack/pallas_call | solution.py:56
  9.0 7.6 %collective-permute-start = (bf16[128,1152]{1,0:T(8,128)(2,1)}, bf16[128,1152]{1,0:T(8,128)(2,1)S(1)}, u32[]{:S(2)}, u32[]{:S(2)}) collective-permute-start(bf16[128,1152]{1,0:T(8,128)(2,1)} %get-tuple-element.33), channel_id=1, source_target_pairs={{0,68},{1,101},{2,198},{3,231},{4,256},{5,289},{6,386},{7,419},{32... | collective-permute-start | bytes 884744 | tf_op jit(solution)/shard_map/ppermute | solution.py:348
  16.6 12.7 %collective-permute-start.1 = (bf16[144,512]{1,0:T(8,128)(2,1)}, bf16[144,512]{1,0:T(8,128)(2,1)S(1)}, u32[]{:S(2)}, u32[]{:S(2)}) collective-permute-start(bf16[144,512]{1,0:T(8,128)(2,1)} %get-tuple-element.52.rest_8_), channel_id=1, source_target_pairs={{0,64},{64,0},{1,65},{65,1},{2,66},{66,2},{3,67},{67,3},{4,68},{68... | collective-permute-start | bytes 442376 | tf_op jit(solution)/shard_map/ppermute | solution.py:356
  29.4 22.3 %collective-permute-start.2 = (bf16[144,512]{1,0:T(8,128)(2,1)}, bf16[144,512]{1,0:T(8,128)(2,1)S(1)}, u32[]{:S(2)}, u32[]{:S(2)}) collective-permute-start(bf16[144,512]{1,0:T(8,128)(2,1)} %get-tuple-element.52.rest_8_), channel_id=1, source_target_pairs={{0,32},{32,0},{1,33},{33,1},{2,34},{34,2},{3,35},{35,3},{4,36},{36... | collective-permute-start | bytes 442376 | tf_op jit(solution)/shard_map/ppermute | solution.py:351
  51.7 1.3 collective-permute-start.3
  53.0 1.6 collective-permute-start.4
  54.6 2.1 collective-permute-start.5
  56.7 1.3 collective-permute-start.6
  58.0 1.9 collective-permute-done.4.rest_5_
  60.0 3.2 %collective-permute-done.5.rest_0_ = bf16[144,512]{1,0:T(8,128)(2,1)S(1)} collective-permute-done((bf16[144,512]{1,0:T(8,128)(2,1)}, bf16[144,512]{1,0:T(8,128)(2,1)S(1)}, u32[]{:S(2)}, u32[]{:S(2)}) %collective-permute-start.5) | collective-permute-done | bytes 147488 | tf_op jit(solution)/shard_map/ppermute | solution.py:353
  63.1 3.2 %collective-permute-done.6.rest_1_ = bf16[144,512]{1,0:T(8,128)(2,1)S(1)} collective-permute-done((bf16[144,512]{1,0:T(8,128)(2,1)}, bf16[144,512]{1,0:T(8,128)(2,1)S(1)}, u32[]{:S(2)}, u32[]{:S(2)}) %collective-permute-start.6) | collective-permute-done | bytes 147488 | tf_op jit(solution)/shard_map/ppermute | solution.py:353
  66.3 2.5 %collective-permute-start.7 = (bf16[144,512]{1,0:T(8,128)(2,1)S(1)}, bf16[144,512]{1,0:T(8,128)(2,1)S(1)}, u32[]{:S(2)}, u32[]{:S(2)}) collective-permute-start(bf16[144,512]{1,0:T(8,128)(2,1)S(1)} %collective-permute-done.1.rest_10_), channel_id=1, source_target_pairs={{0,32},{32,0},{1,33},{33,1},{2,34},{34,2},{3,35},{35,3},{4,36},{36... | collective-permute-start | bytes 442376 | tf_op jit(solution)/shard_map/ppermute | solution.py:351
  68.8 1.3 collective-permute-start.8
  70.1 5.9 %collective-permute-start.9 = (bf16[144,512]{1,0:T(8,128)(2,1)S(1)}, bf16[144,512]{1,0:T(8,128)(2,1)S(1)}, u32[]{:S(2)}, u32[]{:S(2)}) collective-permute-start(bf16[144,512]{1,0:T(8,128)(2,1)S(1)} %collective-permute-done.1.rest_10_), channel_id=1, source_target_pairs={{0,160},{32,128},{128,288},{160,256},{256,416},{288,384},{1,161},{... | collective-permute-start | bytes 442376 | tf_op jit(solution)/shard_map/ppermute | solution.py:353
  76.1 1.9 collective-permute-start.10
  78.0 1.3 collective-permute-start.11
  79.3 0.7 broadcast_in_dim.6.gain_ref
  80.0 0.1 pad_add_fusion.where_ref
  80.1 0.7 copy-done.5
  80.8 0.7 copy-done.6
  81.5 1.2 slots.1
  82.7 3.0 %collective-permute-done.11.rest_3_ = bf16[144,512]{1,0:T(8,128)(2,1)S(1)} collective-permute-done((bf16[144,512]{1,0:T(8,128)(2,1)S(1)}, bf16[144,512]{1,0:T(8,128)(2,1)S(1)}, u32[]{:S(2)}, u32[]{:S(2)}) %collective-permute-start.11) | collective-permute-done | bytes 147488 | tf_op jit(solution)/shard_map/ppermute | solution.py:353
  85.8 0.7 copy-done.1
  86.4 1.0 copy-done.2
  87.5 1.0 copy-done.3
  88.5 0.9 copy-done.4
  89.4 8.5 %attend.1 = (f32[128,2048]{1,0:T(8,128)S(1)}, bf16[1152,2048]{1,0:T(8,128)(2,1)S(1)}) custom-call(s32[4]{0:T(128)S(1)} %pad_add_fusion.where_ref, bf16[128,2048]{1,0:T(8,128)(2,1)S(1)} %bitcast.26, s32[1,128]{1,0:T(1,128)S(1)} %copy-done.1, bf16[128,2048]{1,0:T(8,128)(2,1)S(1)} %bitcast.27, bf16[1,2048]{1,0:T(2,128)(2,1)S(1)} %broadcast_in_dim.6.gain_ref, ...), custom_call_target="tpu_custom_call" | custom-call | flops 1900000000 | bytes 9000000 | tf_op jit(solution)/shard_map/attend/pallas_call | solution.py:176
  97.9 62.9 %all_to_all.22 = bf16[16,72,2048]{2,1,0:T(8,128)(2,1)} all-to-all(bf16[16,72,2048]{2,1,0:T(8,128)(2,1)S(1)} %bitcast.23), channel_id=1, replica_groups=mesh['x'=4,'zh'=2,'c'=2,'y'=4,'zl'=8] {'x','y'}, dimensions={0} | all-to-all | bytes 9437184 | tf_op jit(solution)/shard_map/all_to_all | solution.py:369
  160.9 2.3 copy-done
  163.2 13.1 %expert_mlp.1 = bf16[1152,2048]{1,0:T(8,128)(2,1)S(1)} custom-call(s32[4]{0:T(128)S(1)} %pad_add_fusion.where_ref, bf16[1152,2048]{1,0:T(8,128)(2,1)S(1)} %bitcast.24, bf16[4096,1152]{1,0:T(8,128)(2,1)} %all-gather.2.cloned.1.call-done.w_hbm), custom_call_target="tpu_custom_call" | custom-call | flops 6600000000 | bytes 19000000 | tf_op jit(solution)/shard_map/expert_mlp/pallas_call | solution.py:281
  176.3 57.7 %all_to_all.23 = bf16[16,72,2048]{2,1,0:T(8,128)(2,1)S(1)} all-to-all(bf16[16,72,2048]{2,1,0:T(8,128)(2,1)S(1)} %bitcast.25), channel_id=1, replica_groups=mesh['x'=4,'zh'=2,'c'=2,'y'=4,'zl'=8] {'x','y'}, dimensions={0} | all-to-all | bytes 9437184 | tf_op jit(solution)/shard_map/all_to_all | solution.py:371
  234.0 3.2 %combine.1 = bf16[128,2048]{1,0:T(8,128)(2,1)} custom-call(f32[128,2048]{1,0:T(8,128)S(1)} %get-tuple-element.56.hidden_ref, bf16[128,1152]{1,0:T(8,128)(2,1)S(1)} %get-tuple-element.57.high_ref, bf16[128,1152]{1,0:T(8,128)(2,1)S(1)} %get-tuple-element.58.low_ref, bf16[1152,2048]{1,0:T(8,128)(2,1)S(1)} %bitcast.22), custom_call_target="tpu_custom_call" | custom-call | flops 1200000000 | bytes 7000000 | tf_op jit(solution)/shard_map/combine/pallas_call | solution.py:308
  (20 shorter events, 0.1 us)
Async XLA Ops:
  6.5 154.3 %all-gather.2.cloned.1.call-start = ((), (), s32[]{:S(2)}) async-start(), calls=%async_computation.2 | async-start | bytes 9732096 | tf_op jit(solution)/shard_map/all_gather | solution.py:360
  9.0 20.4 %collective-permute-start = (bf16[128,1152]{1,0:T(8,128)(2,1)}, bf16[128,1152]{1,0:T(8,128)(2,1)S(1)}, u32[]{:S(2)}, u32[]{:S(2)}) collective-permute-start(bf16[128,1152]{1,0:T(8,128)(2,1)} %get-tuple-element.33), channel_id=1, source_target_pairs={{0,68},{1,101},{2,198},{3,231},{4,256},{5,289},{6,386},{7,419},{32... | collective-permute-start | bytes 884744 | tf_op jit(solution)/shard_map/ppermute | solution.py:348
  16.6 40.1 %collective-permute-start.1 = (bf16[144,512]{1,0:T(8,128)(2,1)}, bf16[144,512]{1,0:T(8,128)(2,1)S(1)}, u32[]{:S(2)}, u32[]{:S(2)}) collective-permute-start(bf16[144,512]{1,0:T(8,128)(2,1)} %get-tuple-element.52.rest_8_), channel_id=1, source_target_pairs={{0,64},{64,0},{1,65},{65,1},{2,66},{66,2},{3,67},{67,3},{4,68},{68... | collective-permute-start | bytes 442376 | tf_op jit(solution)/shard_map/ppermute | solution.py:356
  29.4 36.9 %copy-start.7 = (bf16[128,1152]{1,0:T(8,128)(2,1)}, bf16[128,1152]{1,0:T(8,128)(2,1)S(1)}, u32[]{:S(2)}) copy-start(bf16[128,1152]{1,0:T(8,128)(2,1)S(1)} %collective-permute-done) | copy-start | bytes 884740
  29.4 28.6 %collective-permute-start.2 = (bf16[144,512]{1,0:T(8,128)(2,1)}, bf16[144,512]{1,0:T(8,128)(2,1)S(1)}, u32[]{:S(2)}, u32[]{:S(2)}) collective-permute-start(bf16[144,512]{1,0:T(8,128)(2,1)} %get-tuple-element.52.rest_8_), channel_id=1, source_target_pairs={{0,32},{32,0},{1,33},{33,1},{2,34},{34,2},{3,35},{35,3},{4,36},{36... | collective-permute-start | bytes 442376 | tf_op jit(solution)/shard_map/ppermute | solution.py:351
  51.7 6.3 %collective-permute-start.3 = (bf16[144,512]{1,0:T(8,128)(2,1)}, bf16[144,512]{1,0:T(8,128)(2,1)S(1)}, u32[]{:S(2)}, u32[]{:S(2)}) collective-permute-start(bf16[144,512]{1,0:T(8,128)(2,1)} %get-tuple-element.52.rest_8_), channel_id=1, source_target_pairs={{0,128},{32,160},{128,256},{160,288},{256,384},{288,416},{1,129},{... | collective-permute-start | bytes 442376 | tf_op jit(solution)/shard_map/ppermute | solution.py:353
  53.0 6.9 %collective-permute-start.4 = (bf16[144,512]{1,0:T(8,128)(2,1)}, bf16[144,512]{1,0:T(8,128)(2,1)S(1)}, u32[]{:S(2)}, u32[]{:S(2)}) collective-permute-start(bf16[144,512]{1,0:T(8,128)(2,1)} %get-tuple-element.52.rest_8_), channel_id=1, source_target_pairs={{0,160},{32,128},{128,288},{160,256},{256,416},{288,384},{1,161},{... | collective-permute-start | bytes 442376 | tf_op jit(solution)/shard_map/ppermute | solution.py:353
  54.6 8.5 %collective-permute-start.5 = (bf16[144,512]{1,0:T(8,128)(2,1)}, bf16[144,512]{1,0:T(8,128)(2,1)S(1)}, u32[]{:S(2)}, u32[]{:S(2)}) collective-permute-start(bf16[144,512]{1,0:T(8,128)(2,1)} %get-tuple-element.52.rest_8_), channel_id=1, source_target_pairs={{0,256},{32,288},{128,384},{160,416},{1,257},{33,289},{129,385},{1... | collective-permute-start | bytes 442376 | tf_op jit(solution)/shard_map/ppermute | solution.py:353
  56.7 9.6 %collective-permute-start.6 = (bf16[144,512]{1,0:T(8,128)(2,1)}, bf16[144,512]{1,0:T(8,128)(2,1)S(1)}, u32[]{:S(2)}, u32[]{:S(2)}) collective-permute-start(bf16[144,512]{1,0:T(8,128)(2,1)} %get-tuple-element.52.rest_8_), channel_id=1, source_target_pairs={{0,288},{32,256},{128,416},{160,384},{1,289},{33,257},{129,417},{1... | collective-permute-start | bytes 442376 | tf_op jit(solution)/shard_map/ppermute | solution.py:353
  66.3 16.4 %collective-permute-start.7 = (bf16[144,512]{1,0:T(8,128)(2,1)S(1)}, bf16[144,512]{1,0:T(8,128)(2,1)S(1)}, u32[]{:S(2)}, u32[]{:S(2)}) collective-permute-start(bf16[144,512]{1,0:T(8,128)(2,1)S(1)} %collective-permute-done.1.rest_10_), channel_id=1, source_target_pairs={{0,32},{32,0},{1,33},{33,1},{2,34},{34,2},{3,35},{35,3},{4,36},{36... | collective-permute-start | bytes 442376 | tf_op jit(solution)/shard_map/ppermute | solution.py:351
  68.8 13.9 %collective-permute-start.8 = (bf16[144,512]{1,0:T(8,128)(2,1)S(1)}, bf16[144,512]{1,0:T(8,128)(2,1)S(1)}, u32[]{:S(2)}, u32[]{:S(2)}) collective-permute-start(bf16[144,512]{1,0:T(8,128)(2,1)S(1)} %collective-permute-done.1.rest_10_), channel_id=1, source_target_pairs={{0,128},{32,160},{128,256},{160,288},{256,384},{288,416},{1,129},{... | collective-permute-start | bytes 442376 | tf_op jit(solution)/shard_map/ppermute | solution.py:353
  70.1 12.6 %collective-permute-start.9 = (bf16[144,512]{1,0:T(8,128)(2,1)S(1)}, bf16[144,512]{1,0:T(8,128)(2,1)S(1)}, u32[]{:S(2)}, u32[]{:S(2)}) collective-permute-start(bf16[144,512]{1,0:T(8,128)(2,1)S(1)} %collective-permute-done.1.rest_10_), channel_id=1, source_target_pairs={{0,160},{32,128},{128,288},{160,256},{256,416},{288,384},{1,161},{... | collective-permute-start | bytes 442376 | tf_op jit(solution)/shard_map/ppermute | solution.py:353
  76.1 6.7 %collective-permute-start.10 = (bf16[144,512]{1,0:T(8,128)(2,1)S(1)}, bf16[144,512]{1,0:T(8,128)(2,1)S(1)}, u32[]{:S(2)}, u32[]{:S(2)}) collective-permute-start(bf16[144,512]{1,0:T(8,128)(2,1)S(1)} %collective-permute-done.1.rest_10_), channel_id=1, source_target_pairs={{0,256},{32,288},{128,384},{160,416},{1,257},{33,289},{129,385},{1... | collective-permute-start | bytes 442376 | tf_op jit(solution)/shard_map/ppermute | solution.py:353
  78.0 7.8 %collective-permute-start.11 = (bf16[144,512]{1,0:T(8,128)(2,1)S(1)}, bf16[144,512]{1,0:T(8,128)(2,1)S(1)}, u32[]{:S(2)}, u32[]{:S(2)}) collective-permute-start(bf16[144,512]{1,0:T(8,128)(2,1)S(1)} %collective-permute-done.1.rest_10_), channel_id=1, source_target_pairs={{0,288},{32,256},{128,416},{160,384},{1,289},{33,257},{129,417},{1... | collective-permute-start | bytes 442376 | tf_op jit(solution)/shard_map/ppermute | solution.py:353
  80.1 0.7 copy-start.5
  80.8 0.7 copy-start.6
  85.8 0.7 copy-start.1
  86.4 1.0 copy-start.2
  87.5 1.0 copy-start.3
  88.5 0.9 copy-start.4
  160.9 2.3 copy-start
Sparse Core Ops, SparseCore 0:
  66.4 86.1 all-gather.1

commit v4 on v3

--- a/solution.py
+++ b/solution.py
@@ -121,20 +121,22 @@
 
 
 def attention_kernel(where_ref, q_ref, seg_ref, res_ref, gain_ref, send_ref, *rest):
-    blocks = rest[:BLOCKS]
-    hidden_ref, out_ref, kv, segs, bias, hidden = rest[BLOCKS:]
+    blocks = rest[:8]
+    hidden_ref, out_ref, kv, segs, bias, hidden = rest[8:]
     x, zh, c = where_ref[0], where_ref[1], where_ref[2]
-    index = 0
-    for back in (2, 1, 0):
-        for other_zh in (0, 1):
-            for other_c in (0, 1):
+    for other_zh in (0, 1):
+        for other_c in (0, 1):
+            for back in (0, 1, 2):
+                if other_c == 0:
+                    block, top = blocks[other_zh * 3 + back], 0
+                else:
+                    block, top = blocks[6 + other_zh], back * PACK
                 zh_at = zh if other_zh == 0 else 1 - zh
                 c_at = c if other_c == 0 else 1 - c
                 slot = (2 - back) * 4 + zh_at * 2 + c_at
-                kv[pl.ds(pl.multiple_of(slot * TOK, TOK), TOK), :] = blocks[index][:TOK, :]
-                row = blocks[index][TOK:, :TOK].astype(F32)
+                kv[pl.ds(pl.multiple_of(slot * TOK, TOK), TOK), :] = block[top : top + TOK, :]
+                row = block[top + TOK : top + PACK, :TOK].astype(F32)
                 segs[pl.ds(slot, 1), :] = row[:1, :]
-                index += 1
     first = zh * 2 + c
     own = x * 4 + first
     t = lax.broadcasted_iota(jnp.int32, (TOK, TOK), 0)
@@ -175,7 +177,7 @@
     whole = pl.BlockSpec(memory_space=pltpu.VMEM)
     return pl.pallas_call(
         attention_kernel,
-        in_specs=[pl.BlockSpec(memory_space=pltpu.SMEM)] + [whole] * (5 + BLOCKS),
+        in_specs=[pl.BlockSpec(memory_space=pltpu.SMEM)] + [whole] * (5 + 8),
         out_specs=(whole, whole),
         out_shape=(
             jax.ShapeDtypeStruct((TOK, D), F32),
@@ -324,10 +326,8 @@
     )(hidden, high, low, back)
 
 
-def shifted(steps, swap):
-    return [
-        (x * 2 + c, (x + steps) * 2 + (c ^ swap)) for x in range(4) for c in range(2) if x + steps < 4
-    ]
+def shifted(steps):
+    return [(x, x + steps) for x in range(4 - steps)]
 
 
 def to_expert_column():
@@ -348,21 +348,20 @@
     packed = lax.ppermute(packed, ("x", "zh", "c", "zl"), to_expert_column())
 
     def spread(source):
-        found = [[source, lax.ppermute(source, "c", swap)]]
-        for back in (1, 2):
-            found.append([lax.ppermute(source, ("x", "c"), shifted(back, o)) for o in (0, 1)])
-        return found
+        return [source] + [lax.ppermute(source, "x", shifted(back)) for back in (1, 2)]
+
+    def other_core(found):
+        return lax.ppermute(jnp.concatenate(found, axis=0), "c", swap)
 
     packet_zh = lax.ppermute(packet, "zh", swap)
-    packed, packet_near = lax.optimization_barrier((packed, packet))
-    near = spread(packet_near)
-    packed, packet_zh, near = lax.optimization_barrier((packed, packet_zh, near))
-    both = lax.all_gather(packed, ("c", "zh", "zl"), axis=0, tiled=True)
+    near = spread(packet)
+    packet_zh, near = lax.optimization_barrier((packet_zh, near))
     far = spread(packet_zh)
     where = jnp.stack([x, zh, c, y]).astype(jnp.int32)
     ready = (*slot_matrices(where, ids[0].T, gates[0].T), gain[None], seg)
-    far, ready = lax.optimization_barrier((far, ready))
-    blocks = [side[b][o] for b in (2, 1, 0) for side in (near, far) for o in (0, 1)]
+    packed, far, ready = lax.optimization_barrier((packed, far, ready))
+    both = lax.all_gather(packed, ("c", "zh", "zl"), axis=0, tiled=True)
+    blocks = [*near, *far, other_core(near), other_core(far)]
 
     send, high, low, gain_row, seg_row = ready
     hidden, outgoing = attention(where, q[0], seg_row, res[0], gain_row, send, blocks)

time: 247 us -> 222 us (0.90)
  starting transfers between devices: 61.9 us -> 43.4 us
  waiting for transfers between devices: 11.3 us -> 2.37 us
    ppermute x10 -> x6, starting transfers between devices: 41.5 us -> 22.1 us  [the longest x4 13.5 us: spread(): lax.ppermute(source, 'x', shifted(back))]
    ppermute x10 -> x6, waiting for transfers between devices: 11.3 us -> 1.76 us  [the longest x2 1.75 us: other_core(): return lax.ppermute(jnp.concatenate(found, axis=0), 'c', swap)]
    ppermute x1, starting transfers between devices: 12.7 us -> 16.3 us  [body(): packet_zh = lax.ppermute(packet, 'zh', swap)]
    ppermute x1, starting transfers between devices: 7.64 us -> 4.96 us  [body(): packed = lax.ppermute(packed, ('x', 'zh', 'c', 'zl'), to_expert_column())]
  transfers between devices with their start and end apart: 13 -> 9, of which waited for: 4 -> 2; matrix products, arithmetic and copies ran while one was open for 0% -> 1% of each run, Pallas kernels for 4% -> 4%
where the time goes in v4:
time: 222 us; the launch traced here: 220 us
  blocking collectives  122 us (55%)
  starting transfers between devices  43.4 us (20%)
  Pallas kernels  28.5 us (13%)
  between operations  13.5 us (6%)
  local copies, waits for them, and re-layouts  8.76 us (4%)
  waiting for transfers between devices  2.37 us (1%)
    all_to_all x1, blocking collectives, body(): arrived = lax.all_to_all(outgoing, ('x', 'y'), 0, 0, tiled=True)  64.4 us
    all_to_all x1, blocking collectives, body(): back = lax.all_to_all(done, ('x', 'y'), 0, 0, tiled=True)  57.8 us
    ppermute x1, starting transfers between devices, body(): packet_zh = lax.ppermute(packet, 'zh', swap)  16.3 us
    ppermute x4, starting transfers between devices, spread(): lax.ppermute(source, 'x', shifted(back))  13.5 us
    pallas_call x1, Pallas kernels, experts(): pl.pallas_call(expert_kernel, in_specs=[pl.BlockSpec(memory_space=pltpu.S...  13.1 us
    ppermute x2, starting transfers between devices, other_core(): return lax.ppermute(jnp.concatenate(found, axis=0), 'c', swap)  8.63 us
    pallas_call x1, Pallas kernels, attention(): pl.pallas_call(attention_kernel, in_specs=[pl.BlockSpec(memory_space=pltp...  8.53 us
    unnamed x16, local copies, waits for them, and re-layouts  8.06 us
  transfers between devices with their start and end apart: 9, of which 2 were waited for; matrix products, arithmetic and copies ran while one was open for 1% of the time, Pallas kernels for 4%

profile of v4, /device:TPU:1, one launch (start us, length us, event | category | flops | bytes accessed | tf_op | source)
XLA Modules:
  0.0 219.8 jit_solution(306893302959353532)
XLA Ops:
  6.5 2.4 %pack.1 = (bf16[144,512]{1,0:T(8,128)(2,1)}, bf16[128,1152]{1,0:T(8,128)(2,1)}) custom-call(bf16[128,256]{1,0:T(8,128)(2,1)} %bitcast.33, bf16[128,256]{1,0:T(8,128)(2,1)} %bitcast.34, bf16[128,384]{1,0:T(8,128)(2,1)} %bitcast.30, bf16[128,384]{1,0:T(8,128)(2,1)} %bitcast.31, bf16[384,128]{1,0:T(8,128)(2,1)} %bitcast.32, s32[1,128]{1,0:T(1,128)} %seg_ref.2), custom_call_target="tpu_custom_call" | custom-call | bytes 1000000 | tf_op jit(solution)/shard_map/pack/pallas_call | solution.py:56
  9.0 16.3 %collective-permute-start.1 = (bf16[144,512]{1,0:T(8,128)(2,1)}, bf16[144,512]{1,0:T(8,128)(2,1)S(1)}, u32[]{:S(2)}, u32[]{:S(2)}) collective-permute-start(bf16[144,512]{1,0:T(8,128)(2,1)} %get-tuple-element.34.rest_0_), channel_id=1, source_target_pairs={{0,64},{64,0},{1,65},{65,1},{2,66},{66,2},{3,67},{67,3},{4,68},{68... | collective-permute-start | bytes 442376 | tf_op jit(solution)/shard_map/ppermute | solution.py:356
  25.3 3.1 %collective-permute-start.2 = (bf16[144,512]{1,0:T(8,128)(2,1)}, bf16[144,512]{1,0:T(8,128)(2,1)S(1)}, u32[]{:S(2)}, u32[]{:S(2)}) collective-permute-start(bf16[144,512]{1,0:T(8,128)(2,1)} %get-tuple-element.34.rest_0_), channel_id=1, source_target_pairs={{0,128},{128,256},{256,384},{1,129},{129,257},{257,385},{2,130},{1... | collective-permute-start | bytes 442376 | tf_op jit(solution)/shard_map/ppermute | solution.py:351
  28.4 4.4 %collective-permute-start.3 = (bf16[144,512]{1,0:T(8,128)(2,1)}, bf16[144,512]{1,0:T(8,128)(2,1)S(1)}, u32[]{:S(2)}, u32[]{:S(2)}) collective-permute-start(bf16[144,512]{1,0:T(8,128)(2,1)} %get-tuple-element.34.rest_0_), channel_id=1, source_target_pairs={{0,256},{128,384},{1,257},{129,385},{2,258},{130,386},{3,259},{131... | collective-permute-start | bytes 442376 | tf_op jit(solution)/shard_map/ppermute | solution.py:351
  32.8 5.0 %collective-permute-start = (bf16[128,1152]{1,0:T(8,128)(2,1)}, bf16[128,1152]{1,0:T(8,128)(2,1)S(1)}, u32[]{:S(2)}, u32[]{:S(2)}) collective-permute-start(bf16[128,1152]{1,0:T(8,128)(2,1)} %get-tuple-element.25), channel_id=1, source_target_pairs={{0,68},{1,101},{2,198},{3,231},{4,256},{5,289},{6,386},{7,419},{32... | collective-permute-start | bytes 884744 | tf_op jit(solution)/shard_map/ppermute | solution.py:348
  37.8 0.0 collective-permute-done.3.rest_2_
  37.8 2.6 %collective-permute-start.4 = (bf16[144,512]{1,0:T(8,128)(2,1)S(1)}, bf16[144,512]{1,0:T(8,128)(2,1)S(1)}, u32[]{:S(2)}, u32[]{:S(2)}) collective-permute-start(bf16[144,512]{1,0:T(8,128)(2,1)S(1)} %collective-permute-done.1.rest_3_), channel_id=1, source_target_pairs={{0,128},{128,256},{256,384},{1,129},{129,257},{257,385},{2,130},{1... | collective-permute-start | bytes 442376 | tf_op jit(solution)/shard_map/ppermute | solution.py:351
  40.4 3.4 %collective-permute-start.5 = (bf16[144,512]{1,0:T(8,128)(2,1)S(1)}, bf16[144,512]{1,0:T(8,128)(2,1)S(1)}, u32[]{:S(2)}, u32[]{:S(2)}) collective-permute-start(bf16[144,512]{1,0:T(8,128)(2,1)S(1)} %collective-permute-done.1.rest_3_), channel_id=1, source_target_pairs={{0,256},{128,384},{1,257},{129,385},{2,258},{130,386},{3,259},{131... | collective-permute-start | bytes 442376 | tf_op jit(solution)/shard_map/ppermute | solution.py:351
  43.8 0.7 broadcast_in_dim.6.gain_ref
  44.5 0.1 pad_add_fusion.where_ref
  44.6 0.7 copy-done.5
  45.3 0.7 copy-done.6
  46.0 1.2 slots.1
  47.2 0.6 collective-permute-done
  47.7 0.0 collective-permute-done.4.rest_4_
  47.8 0.0 collective-permute-done.5.rest_5_
  47.8 0.7 copy-done.7
  48.5 0.0 all-gather.2.cloned.1.call-update
  48.5 0.9 pad_maximum_fusion
  49.4 6.7 %collective-permute-start.6 = (bf16[432,512]{1,0:T(8,128)(2,1)S(1)}, bf16[432,512]{1,0:T(8,128)(2,1)S(1)}, u32[]{:S(2)}, u32[]{:S(2)}) collective-permute-start(bf16[432,512]{1,0:T(8,128)(2,1)S(1)} %pad_maximum_fusion), channel_id=1, source_target_pairs={{0,32},{32,0},{1,33},{33,1},{2,34},{34,2},{3,35},{35,3},{4,36},{36... | collective-permute-start | bytes 1327112 | tf_op jit(solution)/shard_map/ppermute | solution.py:354
  56.2 1.9 collective-permute-start.7
  58.1 1.7 collective-permute-done.7.rest_7_
  59.9 0.9 copy-done.1
  60.8 0.7 copy-done.2
  61.4 1.0 copy-done.3
  62.5 1.0 copy-done.4
  63.5 8.5 %attend.1 = (f32[128,2048]{1,0:T(8,128)S(1)}, bf16[1152,2048]{1,0:T(8,128)(2,1)S(1)}) custom-call(s32[4]{0:T(128)S(1)} %pad_add_fusion.where_ref, bf16[128,2048]{1,0:T(8,128)(2,1)S(1)} %bitcast.26, s32[1,128]{1,0:T(1,128)S(1)} %copy-done.2, bf16[128,2048]{1,0:T(8,128)(2,1)S(1)} %bitcast.27, bf16[1,2048]{1,0:T(2,128)(2,1)S(1)} %broadcast_in_dim.6.gain_ref, ...), custom_call_target="tpu_custom_call" | custom-call | flops 1900000000 | bytes 9000000 | tf_op jit(solution)/shard_map/attend/pallas_call | solution.py:178
  72.1 64.4 %all_to_all.22 = bf16[16,72,2048]{2,1,0:T(8,128)(2,1)} all-to-all(bf16[16,72,2048]{2,1,0:T(8,128)(2,1)S(1)} %bitcast.23), channel_id=1, replica_groups=mesh['x'=4,'zh'=2,'c'=2,'y'=4,'zl'=8] {'x','y'}, dimensions={0} | all-to-all | bytes 9437184 | tf_op jit(solution)/shard_map/all_to_all | solution.py:368
  136.5 2.3 %copy-done = bf16[16,72,2048]{2,1,0:T(8,128)(2,1)S(1)} copy-done((bf16[16,72,2048]{2,1,0:T(8,128)(2,1)S(1)}, bf16[16,72,2048]{2,1,0:T(8,128)(2,1)}, u32[]{:S(2)}) %copy-start) | copy-done | bytes 4718616
  138.8 13.1 %expert_mlp.1 = bf16[1152,2048]{1,0:T(8,128)(2,1)S(1)} custom-call(s32[4]{0:T(128)S(1)} %pad_add_fusion.where_ref, bf16[1152,2048]{1,0:T(8,128)(2,1)S(1)} %bitcast.24, bf16[4096,1152]{1,0:T(8,128)(2,1)} %all-gather.2.cloned.1.call-done.w_hbm), custom_call_target="tpu_custom_call" | custom-call | flops 6600000000 | bytes 19000000 | tf_op jit(solution)/shard_map/expert_mlp/pallas_call | solution.py:283
  151.9 57.8 %all_to_all.23 = bf16[16,72,2048]{2,1,0:T(8,128)(2,1)S(1)} all-to-all(bf16[16,72,2048]{2,1,0:T(8,128)(2,1)S(1)} %bitcast.25), channel_id=1, replica_groups=mesh['x'=4,'zh'=2,'c'=2,'y'=4,'zl'=8] {'x','y'}, dimensions={0} | all-to-all | bytes 9437184 | tf_op jit(solution)/shard_map/all_to_all | solution.py:370
  209.7 3.2 %combine.1 = bf16[128,2048]{1,0:T(8,128)(2,1)} custom-call(f32[128,2048]{1,0:T(8,128)S(1)} %get-tuple-element.40.hidden_ref, bf16[128,1152]{1,0:T(8,128)(2,1)S(1)} %get-tuple-element.41.high_ref, bf16[128,1152]{1,0:T(8,128)(2,1)S(1)} %get-tuple-element.42.low_ref, bf16[1152,2048]{1,0:T(8,128)(2,1)S(1)} %bitcast.22), custom_call_target="tpu_custom_call" | custom-call | flops 1200000000 | bytes 7000000 | tf_op jit(solution)/shard_map/combine/pallas_call | solution.py:310
  (14 shorter events, 0.1 us)
Async XLA Ops:
  6.5 129.9 %all-gather.2.cloned.1.call-start = ((), (), s32[]{:S(2)}) async-start(), calls=%async_computation.2 | async-start | bytes 9732096 | tf_op jit(solution)/shard_map/all_gather | solution.py:363
  9.0 28.7 %collective-permute-start.1 = (bf16[144,512]{1,0:T(8,128)(2,1)}, bf16[144,512]{1,0:T(8,128)(2,1)S(1)}, u32[]{:S(2)}, u32[]{:S(2)}) collective-permute-start(bf16[144,512]{1,0:T(8,128)(2,1)} %get-tuple-element.34.rest_0_), channel_id=1, source_target_pairs={{0,64},{64,0},{1,65},{65,1},{2,66},{66,2},{3,67},{67,3},{4,68},{68... | collective-permute-start | bytes 442376 | tf_op jit(solution)/shard_map/ppermute | solution.py:356
  25.3 12.5 %collective-permute-start.2 = (bf16[144,512]{1,0:T(8,128)(2,1)}, bf16[144,512]{1,0:T(8,128)(2,1)S(1)}, u32[]{:S(2)}, u32[]{:S(2)}) collective-permute-start(bf16[144,512]{1,0:T(8,128)(2,1)} %get-tuple-element.34.rest_0_), channel_id=1, source_target_pairs={{0,128},{128,256},{256,384},{1,129},{129,257},{257,385},{2,130},{1... | collective-permute-start | bytes 442376 | tf_op jit(solution)/shard_map/ppermute | solution.py:351
  28.4 9.4 %collective-permute-start.3 = (bf16[144,512]{1,0:T(8,128)(2,1)}, bf16[144,512]{1,0:T(8,128)(2,1)S(1)}, u32[]{:S(2)}, u32[]{:S(2)}) collective-permute-start(bf16[144,512]{1,0:T(8,128)(2,1)} %get-tuple-element.34.rest_0_), channel_id=1, source_target_pairs={{0,256},{128,384},{1,257},{129,385},{2,258},{130,386},{3,259},{131... | collective-permute-start | bytes 442376 | tf_op jit(solution)/shard_map/ppermute | solution.py:351
  32.8 15.0 %collective-permute-start = (bf16[128,1152]{1,0:T(8,128)(2,1)}, bf16[128,1152]{1,0:T(8,128)(2,1)S(1)}, u32[]{:S(2)}, u32[]{:S(2)}) collective-permute-start(bf16[128,1152]{1,0:T(8,128)(2,1)} %get-tuple-element.25), channel_id=1, source_target_pairs={{0,68},{1,101},{2,198},{3,231},{4,256},{5,289},{6,386},{7,419},{32... | collective-permute-start | bytes 884744 | tf_op jit(solution)/shard_map/ppermute | solution.py:348
  37.8 10.0 %collective-permute-start.4 = (bf16[144,512]{1,0:T(8,128)(2,1)S(1)}, bf16[144,512]{1,0:T(8,128)(2,1)S(1)}, u32[]{:S(2)}, u32[]{:S(2)}) collective-permute-start(bf16[144,512]{1,0:T(8,128)(2,1)S(1)} %collective-permute-done.1.rest_3_), channel_id=1, source_target_pairs={{0,128},{128,256},{256,384},{1,129},{129,257},{257,385},{2,130},{1... | collective-permute-start | bytes 442376 | tf_op jit(solution)/shard_map/ppermute | solution.py:351
  40.4 7.3 %collective-permute-start.5 = (bf16[144,512]{1,0:T(8,128)(2,1)S(1)}, bf16[144,512]{1,0:T(8,128)(2,1)S(1)}, u32[]{:S(2)}, u32[]{:S(2)}) collective-permute-start(bf16[144,512]{1,0:T(8,128)(2,1)S(1)} %collective-permute-done.1.rest_3_), channel_id=1, source_target_pairs={{0,256},{128,384},{1,257},{129,385},{2,258},{130,386},{3,259},{131... | collective-permute-start | bytes 442376 | tf_op jit(solution)/shard_map/ppermute | solution.py:351
  44.6 0.7 copy-start.5
  45.3 0.7 copy-start.6
  47.7 0.7 copy-start.7
  49.4 8.7 %collective-permute-start.6 = (bf16[432,512]{1,0:T(8,128)(2,1)S(1)}, bf16[432,512]{1,0:T(8,128)(2,1)S(1)}, u32[]{:S(2)}, u32[]{:S(2)}) collective-permute-start(bf16[432,512]{1,0:T(8,128)(2,1)S(1)} %pad_maximum_fusion), channel_id=1, source_target_pairs={{0,32},{32,0},{1,33},{33,1},{2,34},{34,2},{3,35},{35,3},{4,36},{36... | collective-permute-start | bytes 1327112 | tf_op jit(solution)/shard_map/ppermute | solution.py:354
  56.2 3.7 %collective-permute-start.7 = (bf16[432,512]{1,0:T(8,128)(2,1)S(1)}, bf16[432,512]{1,0:T(8,128)(2,1)S(1)}, u32[]{:S(2)}, u32[]{:S(2)}) collective-permute-start(bf16[432,512]{1,0:T(8,128)(2,1)S(1)} %pad_maximum_fusion.1), channel_id=1, source_target_pairs={{0,32},{32,0},{1,33},{33,1},{2,34},{34,2},{3,35},{35,3},{4,36},{36... | collective-permute-start | bytes 1327112 | tf_op jit(solution)/shard_map/ppermute | solution.py:354
  59.9 0.9 copy-start.1
  60.8 0.7 copy-start.2
  61.4 1.0 copy-start.3
  62.5 1.0 copy-start.4
  136.5 2.3 %copy-start = (bf16[16,72,2048]{2,1,0:T(8,128)(2,1)S(1)}, bf16[16,72,2048]{2,1,0:T(8,128)(2,1)}, u32[]{:S(2)}) copy-start(bf16[16,72,2048]{2,1,0:T(8,128)(2,1)} %all_to_all.22) | copy-start | bytes 14155780
Sparse Core Ops, SparseCore 0:
  48.6 84.7 all-gather.1

commit v5 on v4

--- a/solution.py
+++ b/solution.py
@@ -299,10 +299,9 @@
 
 
 def combine_kernel(hidden_ref, high_ref, low_ref, back_ref, out_ref):
-    back = back_ref[...]
-    routed = jnp.dot(high_ref[...], back, preferred_element_type=F32)
-    routed = routed + jnp.dot(low_ref[...], back, preferred_element_type=F32)
-    out_ref[...] = (hidden_ref[...] + routed).astype(BF16)
+    parts = jnp.concatenate([high_ref[...], low_ref[...]], axis=0)
+    routed = jnp.dot(parts, back_ref[...], preferred_element_type=F32)
+    out_ref[...] = (hidden_ref[...] + (routed[:TOK] + routed[TOK:])).astype(BF16)
 
 
 def combine(hidden, high, low, back):

time: 222 us -> 222 us (level)
  no operation moved by 1% of the time
where the time goes in v5:
time: 222 us; the launch traced here: 220 us
  blocking collectives  122 us (55%)
  starting transfers between devices  43.4 us (20%)
  Pallas kernels  28.4 us (13%)
  between operations  13.5 us (6%)
  local copies, waits for them, and re-layouts  8.76 us (4%)
  waiting for transfers between devices  2.37 us (1%)
    all_to_all x1, blocking collectives, body(): arrived = lax.all_to_all(outgoing, ('x', 'y'), 0, 0, tiled=True)  64.4 us
    all_to_all x1, blocking collectives, body(): back = lax.all_to_all(done, ('x', 'y'), 0, 0, tiled=True)  57.8 us
    ppermute x1, starting transfers between devices, body(): packet_zh = lax.ppermute(packet, 'zh', swap)  16.3 us
    ppermute x4, starting transfers between devices, spread(): lax.ppermute(source, 'x', shifted(back))  13.5 us
    pallas_call x1, Pallas kernels, experts(): pl.pallas_call(expert_kernel, in_specs=[pl.BlockSpec(memory_space=pltpu.S...  13.1 us
    ppermute x2, starting transfers between devices, other_core(): return lax.ppermute(jnp.concatenate(found, axis=0), 'c', swap)  8.63 us
    pallas_call x1, Pallas kernels, attention(): pl.pallas_call(attention_kernel, in_specs=[pl.BlockSpec(memory_space=pltp...  8.53 us
    unnamed x16, local copies, waits for them, and re-layouts  8.06 us
  transfers between devices with their start and end apart: 9, of which 2 were waited for; matrix products, arithmetic and copies ran while one was open for 1% of the time, Pallas kernels for 4%

profile of v5, /device:TPU:1, one launch (start us, length us, event | category | flops | bytes accessed | tf_op | source)
XLA Modules:
  0.0 219.7 jit_solution(9905181777501018745)
XLA Ops:
  6.5 2.4 %pack.1 = (bf16[144,512]{1,0:T(8,128)(2,1)}, bf16[128,1152]{1,0:T(8,128)(2,1)}) custom-call(bf16[128,256]{1,0:T(8,128)(2,1)} %bitcast.33, bf16[128,256]{1,0:T(8,128)(2,1)} %bitcast.34, bf16[128,384]{1,0:T(8,128)(2,1)} %bitcast.30, bf16[128,384]{1,0:T(8,128)(2,1)} %bitcast.31, bf16[384,128]{1,0:T(8,128)(2,1)} %bitcast.32, s32[1,128]{1,0:T(1,128)} %seg_ref.2), custom_call_target="tpu_custom_call" | custom-call | bytes 1000000 | tf_op jit(solution)/shard_map/pack/pallas_call | solution.py:56
  9.0 16.3 %collective-permute-start.1 = (bf16[144,512]{1,0:T(8,128)(2,1)}, bf16[144,512]{1,0:T(8,128)(2,1)S(1)}, u32[]{:S(2)}, u32[]{:S(2)}) collective-permute-start(bf16[144,512]{1,0:T(8,128)(2,1)} %get-tuple-element.34.rest_0_), channel_id=1, source_target_pairs={{0,64},{64,0},{1,65},{65,1},{2,66},{66,2},{3,67},{67,3},{4,68},{68... | collective-permute-start | bytes 442376 | tf_op jit(solution)/shard_map/ppermute | solution.py:355
  25.3 3.1 %collective-permute-start.2 = (bf16[144,512]{1,0:T(8,128)(2,1)}, bf16[144,512]{1,0:T(8,128)(2,1)S(1)}, u32[]{:S(2)}, u32[]{:S(2)}) collective-permute-start(bf16[144,512]{1,0:T(8,128)(2,1)} %get-tuple-element.34.rest_0_), channel_id=1, source_target_pairs={{0,128},{128,256},{256,384},{1,129},{129,257},{257,385},{2,130},{1... | collective-permute-start | bytes 442376 | tf_op jit(solution)/shard_map/ppermute | solution.py:350
  28.4 4.4 %collective-permute-start.3 = (bf16[144,512]{1,0:T(8,128)(2,1)}, bf16[144,512]{1,0:T(8,128)(2,1)S(1)}, u32[]{:S(2)}, u32[]{:S(2)}) collective-permute-start(bf16[144,512]{1,0:T(8,128)(2,1)} %get-tuple-element.34.rest_0_), channel_id=1, source_target_pairs={{0,256},{128,384},{1,257},{129,385},{2,258},{130,386},{3,259},{131... | collective-permute-start | bytes 442376 | tf_op jit(solution)/shard_map/ppermute | solution.py:350
  32.8 5.0 %collective-permute-start = (bf16[128,1152]{1,0:T(8,128)(2,1)}, bf16[128,1152]{1,0:T(8,128)(2,1)S(1)}, u32[]{:S(2)}, u32[]{:S(2)}) collective-permute-start(bf16[128,1152]{1,0:T(8,128)(2,1)} %get-tuple-element.25), channel_id=1, source_target_pairs={{0,68},{1,101},{2,198},{3,231},{4,256},{5,289},{6,386},{7,419},{32... | collective-permute-start | bytes 884744 | tf_op jit(solution)/shard_map/ppermute | solution.py:347
  37.8 0.0 collective-permute-done.3.rest_2_
  37.8 2.6 %collective-permute-start.4 = (bf16[144,512]{1,0:T(8,128)(2,1)S(1)}, bf16[144,512]{1,0:T(8,128)(2,1)S(1)}, u32[]{:S(2)}, u32[]{:S(2)}) collective-permute-start(bf16[144,512]{1,0:T(8,128)(2,1)S(1)} %collective-permute-done.1.rest_3_), channel_id=1, source_target_pairs={{0,128},{128,256},{256,384},{1,129},{129,257},{257,385},{2,130},{1... | collective-permute-start | bytes 442376 | tf_op jit(solution)/shard_map/ppermute | solution.py:350
  40.4 3.4 %collective-permute-start.5 = (bf16[144,512]{1,0:T(8,128)(2,1)S(1)}, bf16[144,512]{1,0:T(8,128)(2,1)S(1)}, u32[]{:S(2)}, u32[]{:S(2)}) collective-permute-start(bf16[144,512]{1,0:T(8,128)(2,1)S(1)} %collective-permute-done.1.rest_3_), channel_id=1, source_target_pairs={{0,256},{128,384},{1,257},{129,385},{2,258},{130,386},{3,259},{131... | collective-permute-start | bytes 442376 | tf_op jit(solution)/shard_map/ppermute | solution.py:350
  43.8 0.7 broadcast_in_dim.6.gain_ref
  44.5 0.1 pad_add_fusion.where_ref
  44.6 0.7 copy-done.5
  45.3 0.7 copy-done.6
  46.0 1.2 slots.1
  47.2 0.6 collective-permute-done
  47.7 0.0 collective-permute-done.4.rest_4_
  47.8 0.0 collective-permute-done.5.rest_5_
  47.8 0.7 copy-done.7
  48.5 0.0 all-gather.2.cloned.1.call-update
  48.5 0.9 pad_maximum_fusion
  49.4 6.7 %collective-permute-start.6 = (bf16[432,512]{1,0:T(8,128)(2,1)S(1)}, bf16[432,512]{1,0:T(8,128)(2,1)S(1)}, u32[]{:S(2)}, u32[]{:S(2)}) collective-permute-start(bf16[432,512]{1,0:T(8,128)(2,1)S(1)} %pad_maximum_fusion), channel_id=1, source_target_pairs={{0,32},{32,0},{1,33},{33,1},{2,34},{34,2},{3,35},{35,3},{4,36},{36... | collective-permute-start | bytes 1327112 | tf_op jit(solution)/shard_map/ppermute | solution.py:353
  56.2 1.9 collective-permute-start.7
  58.1 1.7 collective-permute-done.7.rest_7_
  59.9 0.9 copy-done.1
  60.8 0.7 copy-done.2
  61.4 1.0 copy-done.3
  62.5 1.0 copy-done.4
  63.5 8.5 %attend.1 = (f32[128,2048]{1,0:T(8,128)S(1)}, bf16[1152,2048]{1,0:T(8,128)(2,1)S(1)}) custom-call(s32[4]{0:T(128)S(1)} %pad_add_fusion.where_ref, bf16[128,2048]{1,0:T(8,128)(2,1)S(1)} %bitcast.26, s32[1,128]{1,0:T(1,128)S(1)} %copy-done.2, bf16[128,2048]{1,0:T(8,128)(2,1)S(1)} %bitcast.27, bf16[1,2048]{1,0:T(2,128)(2,1)S(1)} %broadcast_in_dim.6.gain_ref, ...), custom_call_target="tpu_custom_call" | custom-call | flops 1900000000 | bytes 9000000 | tf_op jit(solution)/shard_map/attend/pallas_call | solution.py:178
  72.1 64.4 %all_to_all.22 = bf16[16,72,2048]{2,1,0:T(8,128)(2,1)} all-to-all(bf16[16,72,2048]{2,1,0:T(8,128)(2,1)S(1)} %bitcast.23), channel_id=1, replica_groups=mesh['x'=4,'zh'=2,'c'=2,'y'=4,'zl'=8] {'x','y'}, dimensions={0} | all-to-all | bytes 9437184 | tf_op jit(solution)/shard_map/all_to_all | solution.py:367
  136.5 2.3 %copy-done = bf16[16,72,2048]{2,1,0:T(8,128)(2,1)S(1)} copy-done((bf16[16,72,2048]{2,1,0:T(8,128)(2,1)S(1)}, bf16[16,72,2048]{2,1,0:T(8,128)(2,1)}, u32[]{:S(2)}) %copy-start) | copy-done | bytes 4718616
  138.8 13.1 %expert_mlp.1 = bf16[1152,2048]{1,0:T(8,128)(2,1)S(1)} custom-call(s32[4]{0:T(128)S(1)} %pad_add_fusion.where_ref, bf16[1152,2048]{1,0:T(8,128)(2,1)S(1)} %bitcast.24, bf16[4096,1152]{1,0:T(8,128)(2,1)} %all-gather.2.cloned.1.call-done.w_hbm), custom_call_target="tpu_custom_call" | custom-call | flops 6600000000 | bytes 19000000 | tf_op jit(solution)/shard_map/expert_mlp/pallas_call | solution.py:283
  151.9 57.8 %all_to_all.23 = bf16[16,72,2048]{2,1,0:T(8,128)(2,1)S(1)} all-to-all(bf16[16,72,2048]{2,1,0:T(8,128)(2,1)S(1)} %bitcast.25), channel_id=1, replica_groups=mesh['x'=4,'zh'=2,'c'=2,'y'=4,'zl'=8] {'x','y'}, dimensions={0} | all-to-all | bytes 9437184 | tf_op jit(solution)/shard_map/all_to_all | solution.py:369
  209.7 3.2 %combine.1 = bf16[128,2048]{1,0:T(8,128)(2,1)} custom-call(f32[128,2048]{1,0:T(8,128)S(1)} %get-tuple-element.40.hidden_ref, bf16[128,1152]{1,0:T(8,128)(2,1)S(1)} %get-tuple-element.41.high_ref, bf16[128,1152]{1,0:T(8,128)(2,1)S(1)} %get-tuple-element.42.low_ref, bf16[1152,2048]{1,0:T(8,128)(2,1)S(1)} %bitcast.22), custom_call_target="tpu_custom_call" | custom-call | flops 1200000000 | bytes 7000000 | tf_op jit(solution)/shard_map/combine/pallas_call | solution.py:309
  (14 shorter events, 0.1 us)
Async XLA Ops:
  6.5 129.9 %all-gather.2.cloned.1.call-start = ((), (), s32[]{:S(2)}) async-start(), calls=%async_computation.2 | async-start | bytes 9732096 | tf_op jit(solution)/shard_map/all_gather | solution.py:362
  9.0 28.7 %collective-permute-start.1 = (bf16[144,512]{1,0:T(8,128)(2,1)}, bf16[144,512]{1,0:T(8,128)(2,1)S(1)}, u32[]{:S(2)}, u32[]{:S(2)}) collective-permute-start(bf16[144,512]{1,0:T(8,128)(2,1)} %get-tuple-element.34.rest_0_), channel_id=1, source_target_pairs={{0,64},{64,0},{1,65},{65,1},{2,66},{66,2},{3,67},{67,3},{4,68},{68... | collective-permute-start | bytes 442376 | tf_op jit(solution)/shard_map/ppermute | solution.py:355
  25.3 12.5 %collective-permute-start.2 = (bf16[144,512]{1,0:T(8,128)(2,1)}, bf16[144,512]{1,0:T(8,128)(2,1)S(1)}, u32[]{:S(2)}, u32[]{:S(2)}) collective-permute-start(bf16[144,512]{1,0:T(8,128)(2,1)} %get-tuple-element.34.rest_0_), channel_id=1, source_target_pairs={{0,128},{128,256},{256,384},{1,129},{129,257},{257,385},{2,130},{1... | collective-permute-start | bytes 442376 | tf_op jit(solution)/shard_map/ppermute | solution.py:350
  28.4 9.4 %collective-permute-start.3 = (bf16[144,512]{1,0:T(8,128)(2,1)}, bf16[144,512]{1,0:T(8,128)(2,1)S(1)}, u32[]{:S(2)}, u32[]{:S(2)}) collective-permute-start(bf16[144,512]{1,0:T(8,128)(2,1)} %get-tuple-element.34.rest_0_), channel_id=1, source_target_pairs={{0,256},{128,384},{1,257},{129,385},{2,258},{130,386},{3,259},{131... | collective-permute-start | bytes 442376 | tf_op jit(solution)/shard_map/ppermute | solution.py:350
  32.8 15.0 %collective-permute-start = (bf16[128,1152]{1,0:T(8,128)(2,1)}, bf16[128,1152]{1,0:T(8,128)(2,1)S(1)}, u32[]{:S(2)}, u32[]{:S(2)}) collective-permute-start(bf16[128,1152]{1,0:T(8,128)(2,1)} %get-tuple-element.25), channel_id=1, source_target_pairs={{0,68},{1,101},{2,198},{3,231},{4,256},{5,289},{6,386},{7,419},{32... | collective-permute-start | bytes 884744 | tf_op jit(solution)/shard_map/ppermute | solution.py:347
  37.8 10.0 %collective-permute-start.4 = (bf16[144,512]{1,0:T(8,128)(2,1)S(1)}, bf16[144,512]{1,0:T(8,128)(2,1)S(1)}, u32[]{:S(2)}, u32[]{:S(2)}) collective-permute-start(bf16[144,512]{1,0:T(8,128)(2,1)S(1)} %collective-permute-done.1.rest_3_), channel_id=1, source_target_pairs={{0,128},{128,256},{256,384},{1,129},{129,257},{257,385},{2,130},{1... | collective-permute-start | bytes 442376 | tf_op jit(solution)/shard_map/ppermute | solution.py:350
  40.4 7.3 %collective-permute-start.5 = (bf16[144,512]{1,0:T(8,128)(2,1)S(1)}, bf16[144,512]{1,0:T(8,128)(2,1)S(1)}, u32[]{:S(2)}, u32[]{:S(2)}) collective-permute-start(bf16[144,512]{1,0:T(8,128)(2,1)S(1)} %collective-permute-done.1.rest_3_), channel_id=1, source_target_pairs={{0,256},{128,384},{1,257},{129,385},{2,258},{130,386},{3,259},{131... | collective-permute-start | bytes 442376 | tf_op jit(solution)/shard_map/ppermute | solution.py:350
  44.6 0.7 copy-start.5
  45.3 0.7 copy-start.6
  47.7 0.7 copy-start.7
  49.4 8.7 %collective-permute-start.6 = (bf16[432,512]{1,0:T(8,128)(2,1)S(1)}, bf16[432,512]{1,0:T(8,128)(2,1)S(1)}, u32[]{:S(2)}, u32[]{:S(2)}) collective-permute-start(bf16[432,512]{1,0:T(8,128)(2,1)S(1)} %pad_maximum_fusion), channel_id=1, source_target_pairs={{0,32},{32,0},{1,33},{33,1},{2,34},{34,2},{3,35},{35,3},{4,36},{36... | collective-permute-start | bytes 1327112 | tf_op jit(solution)/shard_map/ppermute | solution.py:353
  56.2 3.7 %collective-permute-start.7 = (bf16[432,512]{1,0:T(8,128)(2,1)S(1)}, bf16[432,512]{1,0:T(8,128)(2,1)S(1)}, u32[]{:S(2)}, u32[]{:S(2)}) collective-permute-start(bf16[432,512]{1,0:T(8,128)(2,1)S(1)} %pad_maximum_fusion.1), channel_id=1, source_target_pairs={{0,32},{32,0},{1,33},{33,1},{2,34},{34,2},{3,35},{35,3},{4,36},{36... | collective-permute-start | bytes 1327112 | tf_op jit(solution)/shard_map/ppermute | solution.py:353
  59.9 0.9 copy-start.1
  60.8 0.7 copy-start.2
  61.4 1.0 copy-start.3
  62.5 1.0 copy-start.4
  136.5 2.3 %copy-start = (bf16[16,72,2048]{2,1,0:T(8,128)(2,1)S(1)}, bf16[16,72,2048]{2,1,0:T(8,128)(2,1)}, u32[]{:S(2)}) copy-start(bf16[16,72,2048]{2,1,0:T(8,128)(2,1)} %all_to_all.22) | copy-start | bytes 14155780
Sparse Core Ops, SparseCore 0:
  48.6 84.7 all-gather.1
